TPU v7x, 32 devices: a whole 2x2x4 slice. The times are simulated.
32 devices in a mesh: pw: 2 (over x), band: 16 (over z, y, core).
Axes of the slice: x: 2, y: 2, z: 4, core: 2. Of those that a mesh axis runs over, the one named last changes fastest.
Arguments:
- stick_coefs: float32 [16, 2, 48, 256], P('band', None, None, 'pw'), may hold values from -6 to 6
- miller: int32 [2, 256], P(None, 'pw'), may hold values from 0 to 47, as said below
- stick_count: int32 [2], P('pw'), may hold values from 1 to 128, as said below
Outputs:
- exchange_coefs: float32 [16, 2, 48, 256], P('band', None, None, 'pw')
Inputs may be any that keep to these rules, and one draw needn't show every extreme that they name: `stick_count`: some pw index has exactly 128 live sticks. Over the live slots the columns (miller[0, s], miller[1, s]) are distinct and are the columns of smallest sigma(miller[0])**2 + sigma(miller[1])**2, as many as there are live slots (ties at the edge broken arbitrarily); the other slots hold arbitrary columns.
All inputs are finite; a program needn't handle non-finite values.
Results may differ from a plain program's by a relative error of at most 0.0003.
Values sent between devices are 32-bit elements; how exact they have to be, the bound alone decides.
No kernel may reach another device: no remote copies, remote signals or barrier semaphores. Data moves between devices by JAX's collectives and lax.ppermute only.
A program may use at most 64 MiB of HBM per device.

v0:
```python
import functools
import math

import jax
import jax.numpy as jnp
import ml_dtypes
import numpy as np
from jax import lax
from jax.experimental import pallas as pl
from jax.experimental.pallas import tpu as pltpu
from jax.sharding import PartitionSpec as P

HALF = 2
kernel_scale = 4.0
screen_width = 16.0
LANES = 128
ROWS = 16


def round_up(value, unit):
    return -(-value // unit) * unit


def split_table(table):
    head = table.astype(np.float32).astype(ml_dtypes.bfloat16)
    rest = (table - head.astype(np.float64)).astype(np.float32).astype(ml_dtypes.bfloat16)
    return head, rest


@functools.lru_cache(maxsize=None)
def build_tables(points, sticks, members):
    signed = np.arange(points)
    signed = np.where(signed < points // 2, signed, signed - points)
    radius = signed[:, None] ** 2 + signed[None, :] ** 2
    limit = np.sort(radius.reshape(-1))[min(sticks, points * points) - 1]
    picked = sorted({(abs(b), abs(c)) for b in signed for c in signed if b * b + c * c <= limit})
    largest = max(b for b, _ in picked)
    grid = 4 * largest + 1 if 4 * largest + 1 < points else points

    def fold(value):
        value = value % points
        return min(value, points - value)

    pairs = set()
    for b1, c1 in picked:
        for b2, c2 in picked:
            for b in {fold(b1 + b2), fold(b1 - b2)}:
                for c in {fold(c1 + c2), fold(c1 - c2)}:
                    pairs.add((b, c))
    pairs = sorted(pairs)
    near = grid // 2 + 1
    place = [(y, z) for y in range(near) for z in range(near)]
    once = np.array([0.5 if 2 * y % grid == 0 else 1.0 for y in range(near)])
    place_weight = np.array([once[y] * once[z] for y, z in place])

    def wave(kind, freq, spot):
        angle = 2.0 * np.pi * ((freq[:, None] * spot[None, :]) % grid) / grid
        return np.cos(angle) if kind == "c" else np.sin(angle)

    spots = np.array(place)

    def class_waves(freqs):
        freqs = np.array(freqs)
        return [
            wave(ky, freqs[:, 0], spots[:, 0]) * wave(kz, freqs[:, 1], spots[:, 1])
            for ky, kz in ("cc", "sc", "cs", "ss")
        ]

    n_place = round_up(len(place), ROWS)
    n_pairs = round_up(len(pairs), ROWS)
    n_picked = round_up(len(picked), ROWS)

    def stack(tables, rows, cols):
        head = np.zeros((4, rows, 3 * cols), ml_dtypes.bfloat16)
        for at, table in enumerate(tables):
            full = np.zeros((rows, cols))
            full[: table.shape[0], : table.shape[1]] = table
            high, low = split_table(full)
            head[at] = np.concatenate([high, high, low], axis=1)
        return head

    scale = points**-1.5
    small = class_waves(picked)
    large = class_waves(pairs)
    synth = stack([t.T * scale for t in small], n_place, n_picked)
    project = stack(
        [-t * place_weight * scale * (points / grid) ** 2 for t in small], n_picked, n_place
    )
    forward = stack([t * place_weight for t in large], n_pairs, n_place)
    inverse = stack([t.T for t in large], n_place, n_pairs)

    index = np.arange(points)
    angle = 2.0 * np.pi * ((index[:, None] * index[None, :]) % points) / points
    cas = np.cos(angle) + np.sin(angle)
    lanes = round_up(members * points, LANES)
    block = np.zeros((lanes, lanes))
    for member in range(members):
        at = member * points
        block[at : at + points, at : at + points] = cas
    high, low = split_table(block)
    turn_left = np.concatenate([high, high, low], axis=1)
    turn_right = np.block([[high, low], [high, low]])

    squares = signed.astype(np.float64) ** 2
    freqs = np.array(pairs)
    total = (freqs[:, 0] ** 2 + freqs[:, 1] ** 2)[:, None] + squares[None, :]
    scaled = total / screen_width
    safe = np.where(total > 0, scaled, 1.0)
    kernel = kernel_scale * np.where(total > 0, -np.expm1(-safe) / safe, 1.0)
    double = np.where(2 * freqs % grid == 0, 1.0, 2.0)
    kernel = kernel * (double[:, 0] * double[:, 1])[:, None]
    kernel = kernel * (points / grid) ** 2 / float(points**3)
    weights = np.zeros((n_pairs, lanes), np.float32)
    for member in range(members):
        weights[: len(pairs), member * points : (member + 1) * points] = kernel

    codes = np.full((n_picked, LANES), -7.0, np.float32)
    for at, (b, c) in enumerate(picked):
        codes[at] = b * points + c
    return dict(
        synth=synth,
        project=project,
        forward=forward,
        inverse=inverse,
        turn_left=turn_left,
        turn_right=turn_right,
        weights=weights,
        codes=codes,
    )


TABLE_NAMES = (
    "synth",
    "project",
    "forward",
    "inverse",
    "turn_left",
    "turn_right",
    "weights",
    "codes",
)


def dot(left, right):
    return jnp.dot(left, right, preferred_element_type=jnp.float32)


def split(value):
    high = value.astype(jnp.bfloat16)
    low = (value - high.astype(jnp.float32)).astype(jnp.bfloat16)
    return high, low


def stacked(value):
    high, low = split(value)
    return jnp.concatenate([high, low, high], axis=0)


def pick_matrix(indices, codes, points):
    first, second = indices[0:1], indices[1:2]
    alive = first >= 0.0
    signed_first = jnp.where(first < points // 2, first, first - points)
    signed_second = jnp.where(second < points // 2, second, second - points)
    code = jnp.abs(signed_first) * points + jnp.abs(signed_second)
    code = jnp.where(alive, code, -1.0)
    one = jnp.where(codes[:, 0:1] == code, 1.0, 0.0)
    sign_first = jnp.where(signed_first < 0.0, -1.0, 1.0)
    sign_second = jnp.where(signed_second < 0.0, -1.0, 1.0)
    parts = [one, one * sign_first, one * sign_second, one * (sign_first * sign_second)]
    return jnp.concatenate(parts, axis=0).astype(jnp.bfloat16)


def unfold(parts):
    even, odd = parts[0] + parts[2], parts[1] + parts[3]
    even_less, odd_less = parts[0] - parts[2], parts[1] - parts[3]
    return [even + odd, even - odd, even_less + odd_less, even_less - odd_less]


def turn(value, turn_right):
    lanes = turn_right.shape[0] // 2
    outs = []
    for at in range(0, value.shape[1], lanes):
        high, low = split(value[:, at : at + lanes])
        out = dot(jnp.concatenate([high, low], axis=1), turn_right)
        outs.append(out[:, :lanes] + out[:, lanes:])
    return outs[0] if len(outs) == 1 else jnp.concatenate(outs, axis=1)


def each_part(small, body):
    if small:
        for at in range(4):
            body(at)
    else:
        pl.loop(0, 4)(body)


def synthesize(small, blocks, pick, turn_left, synth_ref, coefs_ref, orbs_ref):
    fields = [dot(turn_left, stacked(block)) for block in blocks]
    field = fields[0] if len(fields) == 1 else jnp.concatenate(fields, axis=0)
    high, low = split(field)
    contract = (((1,), (1,)), ((), ()))
    coefs = lax.dot_general(pick, high, contract, preferred_element_type=jnp.float32)
    coefs = coefs + lax.dot_general(pick, low, contract, preferred_element_type=jnp.float32)
    rows = pick.shape[0] // 4
    for at in range(4):
        coefs_ref[at] = coefs[at * rows : (at + 1) * rows]

    def body(at):
        orbs_ref[at] = dot(synth_ref[at], stacked(coefs_ref[at]))

    each_part(small, body)
    for at, quadrant in enumerate(unfold([orbs_ref[at] for at in range(4)])):
        orbs_ref[at] = quadrant


def exchange_kernel(
    members,
    points,
    group_blocks,
    indices_ref,
    *refs,
):
    count = sum(group_blocks)
    coef_refs = refs[:count]
    tables = refs[count : count + len(TABLE_NAMES)]
    synth_ref, project_ref, forward_ref, inverse_ref = tables[:4]
    turn_left_ref, turn_right_ref, weights_ref, codes_ref = tables[4:]
    out_ref, own_ref, visit_ref, field_ref, work_ref, coefs_ref = refs[count + len(TABLE_NAMES) :]
    pick = pick_matrix(indices_ref[...], codes_ref[...], points)
    turn_left, turn_right = turn_left_ref[...], turn_right_ref[...]
    lanes = turn_right.shape[0] // 2
    pad = lanes - members * points
    small = forward_ref.shape[1] <= 512

    def coefs_of(ref):
        block = jnp.concatenate([ref[at] for at in range(ref.shape[0])], axis=1)
        if pad:
            block = jnp.concatenate([block, jnp.zeros((pad, block.shape[1]), block.dtype)], axis=0)
        return block

    synthesize(
        small,
        [coefs_of(coef_refs[0])],
        pick,
        turn_left,
        synth_ref,
        coefs_ref.at[:, :, :lanes],
        own_ref,
    )
    field_ref[...] = jnp.zeros_like(field_ref)
    start = 0
    for size in group_blocks:
        blocks = [coefs_of(ref) for ref in coef_refs[start : start + size]]
        start += size
        wide = size * lanes
        visit, work = visit_ref.at[:, :, :wide], work_ref.at[:, :, :wide]
        synthesize(small, blocks, pick, turn_left, synth_ref, coefs_ref.at[:, :, :wide], visit)

        density = []
        for at in range(4):
            own = own_ref[at]
            both = own if size == 1 else jnp.concatenate([own] * size, axis=1)
            density.append(both * visit[at])
        for at, part in enumerate(unfold(density)):
            work[at] = part

        def poisson(at):
            spectrum = dot(forward_ref[at], stacked(work[at]))
            spectrum = turn(spectrum, turn_right)
            weights = weights_ref[...]
            weights = weights if size == 1 else jnp.concatenate([weights] * size, axis=1)
            spectrum = turn(spectrum * weights, turn_right)
            work[at] = dot(inverse_ref[at], stacked(spectrum))

        each_part(small, poisson)
        for at, quadrant in enumerate(unfold([work[at] for at in range(4)])):
            term = quadrant * visit[at]
            total = term[:, :lanes]
            for block in range(1, size):
                total = total + term[:, block * lanes : (block + 1) * lanes]
            field_ref[at] += total

    field = unfold([field_ref[at] for at in range(4)])
    coefs = [dot(project_ref[at], stacked(field[at])) for at in range(4)]
    coefs = turn(jnp.concatenate(coefs, axis=0), turn_right)
    high, low = split(coefs.T)
    own_pick = pick[:, : out_ref.shape[1]]
    result = dot(high, own_pick) + dot(low, own_pick)
    out_ref[...] = result[: members * points]


def swap(value, axis, partner):
    count = lax.axis_size(axis)
    return lax.ppermute(value, axis, [(at, partner(at) % count) for at in range(count)])


def rest_of_ring(value, axis):
    count = lax.axis_size(axis)
    return [
        lax.ppermute(value, axis, [(at, (at + step) % count) for at in range(count)])
        for step in range(1, count)
    ]


def shards(stick_coefs, miller, stick_count):
    groups, members, points, per_owner = stick_coefs.shape
    owners = lax.axis_size("pw")
    batch = max(n for n in range(1, members + 1) if members % n == 0 and (n == 1 or n * points <= LANES))
    tables = build_tables(points, per_owner * owners, batch)
    position = jnp.arange(per_owner, dtype=jnp.int32)[None]
    indices = jnp.where(position < stick_count[0], miller, -1).astype(jnp.float32)
    own = stick_coefs.reshape(members * points, per_owner)
    load = jnp.concatenate([own, indices, jnp.zeros((6, per_owner), jnp.float32)], axis=0)
    loads = [load] + rest_of_ring(load, "pw")
    coefs = jnp.stack([part[: members * points] for part in loads])
    indices = jnp.concatenate([part[members * points :] for part in loads], axis=1)

    ring = lax.axis_size("band")
    mate = swap(coefs, "band", lambda at: at ^ 1)
    near = swap(coefs, "band", lambda at: at ^ 2)
    far = swap(coefs, "band", lambda at: at + 2 if at & 2 else at - 2 + ring)
    me = lax.axis_index("band")
    near_goes = (me & 1) == ((me >> 1) & 1)
    last = swap(jnp.where(near_goes, near, far), "band", lambda at: at ^ 1)

    lanes = tables["turn_right"].shape[0] // 2
    n_place, n_picked = tables["synth"].shape[1], tables["project"].shape[1]
    blocks = (2, 2, 1)
    vmem = pl.BlockSpec(memory_space=pltpu.VMEM)
    values = [jnp.asarray(tables[name]) for name in TABLE_NAMES]

    def exchange(pieces):
        return pl.pallas_call(
            functools.partial(exchange_kernel, batch, points, blocks),
            out_shape=jax.ShapeDtypeStruct((batch * points, per_owner), jnp.float32),
            in_specs=[vmem] * (1 + len(pieces) + len(values)),
            out_specs=vmem,
            scratch_shapes=[
                pltpu.VMEM((4, n_place, lanes), jnp.float32),
                pltpu.VMEM((4, n_place, 2 * lanes), jnp.float32),
                pltpu.VMEM((4, n_place, lanes), jnp.float32),
                pltpu.VMEM((4, n_place, 2 * lanes), jnp.float32),
                pltpu.VMEM((4, n_picked, 2 * lanes), jnp.float32),
            ],
            compiler_params=pltpu.CompilerParams(vmem_limit_bytes=50 * 2**20),
        )(indices, *pieces, *values)

    pieces = (coefs, mate, near, far, last)
    if batch == members:
        result = exchange(pieces)
    else:
        cut = lambda piece: piece.reshape(owners, -1, batch * points, per_owner).swapaxes(0, 1)
        result = lax.map(exchange, tuple(cut(piece) for piece in pieces))
    return result.reshape(groups, members, points, per_owner)


def solution(mesh):
    return jax.shard_map(
        shards,
        mesh=mesh,
        in_specs=(P("band", None, None, "pw"), P(None, "pw"), P("pw")),
        out_specs=P("band", None, None, "pw"),
        check_vma=False,
    )
```

profile of v0, /device:TPU:1, one launch (start us, length us, event | category | flops | bytes accessed | tf_op | source)
XLA Modules:
  0.0 41.6 jit_solution(1185418111725360493)
XLA Ops:
  0.7 0.7 %select_convert_fusion = f32[2,128]{1,0:T(2,128)S(1)} fusion(s32[2,128]{1,0:T(2,128)} %param.12, pred[128]{0:T(512)(128)(4,1)S(1)} %iota_compare_fusion.1), kind=kLoop, calls=%fused_computation.6 | loop fusion | flops 512 | bytes 2176 | tf_op jit(solution)/shard_map/convert_element_type | solution.py:311
  1.4 0.1 pad.7.clone
  1.4 0.9 %maximum_maximum_fusion = f32[104,128]{1,0:T(8,128)S(1)} fusion(f32[2,128]{1,0:T(2,128)S(1)} %select_convert_fusion, f32[96,128]{1,0:T(8,128)} %bitcast.7, f32[104]{0:T(128)S(1)} %pad.7.clone), kind=kLoop, calls=%fused_computation.1 | loop fusion | flops 26624 | bytes 103840 | tf_op jit(solution)/shard_map/concatenate | solution.py:313
  2.3 2.1 %collective-permute-start = (f32[104,128]{1,0:T(8,128)S(1)}, f32[104,128]{1,0:T(8,128)S(1)}, u32[]{:S(2)}, u32[]{:S(2)}) collective-permute-start(f32[104,128]{1,0:T(8,128)S(1)} %maximum_maximum_fusion), channel_id=1, source_target_pairs={{0,16},{16,0},{1,17},{17,1},{2,18},{18,2},{3,19},{19,3},{4,20},{20... | collective-permute-start | bytes 159752 | tf_op jit(solution)/shard_map/ppermute | solution.py:300
  4.4 1.5 %collective-permute-done = f32[104,128]{1,0:T(8,128)S(1)} collective-permute-done((f32[104,128]{1,0:T(8,128)S(1)}, f32[104,128]{1,0:T(8,128)S(1)}, u32[]{:S(2)}, u32[]{:S(2)}) %collective-permute-start) | collective-permute-done | bytes 53280 | tf_op jit(solution)/shard_map/ppermute | solution.py:300
  5.9 0.8 %pad_maximum_fusion.refs_0_ = f32[2,96,128]{2,1,0:T(8,128)S(1)} fusion(f32[1,96,128]{2,1,0:T(8,128)S(1)} %slice_bitcast_fusion, f32[1,96,128]{2,1,0:T(8,128)} %bitcast.8), kind=kLoop, calls=%fused_computation | loop fusion | flops 24576 | bytes 196608 | tf_op jit(solution)/shard_map/stack | solution.py:315
  6.8 4.5 %collective-permute-start.3 = (f32[2,96,128]{2,1,0:T(8,128)S(1)}, f32[2,96,128]{2,1,0:T(8,128)S(1)}, u32[]{:S(2)}, u32[]{:S(2)}) collective-permute-start(f32[2,96,128]{2,1,0:T(8,128)S(1)} %pad_maximum_fusion.refs_0_), channel_id=1, source_target_pairs={{0,14},{1,15},{2,4},{3,5},{4,2},{5,3},{6,8},{7,9},{8,6},{9,7},{10,... | collective-permute-start | bytes 294920 | tf_op jit(solution)/shard_map/ppermute | solution.py:294
  11.3 0.0 collective-permute-start.2
  11.3 2.1 %collective-permute-start.1 = (f32[2,96,128]{2,1,0:T(8,128)S(1)}, f32[2,96,128]{2,1,0:T(8,128)S(1)}, u32[]{:S(2)}, u32[]{:S(2)}) collective-permute-start(f32[2,96,128]{2,1,0:T(8,128)S(1)} %pad_maximum_fusion.refs_0_), channel_id=1, source_target_pairs={{0,1},{1,0},{2,3},{3,2},{4,5},{5,4},{6,7},{7,6},{8,9},{9,8},{10,11... | collective-permute-start | bytes 294920 | tf_op jit(solution)/shard_map/ppermute | solution.py:294
  13.4 0.0 collective-permute-done.3.refs_3_
  13.4 2.4 %collective-permute-done.2.refs_2_ = f32[2,96,128]{2,1,0:T(8,128)S(1)} collective-permute-done((f32[2,96,128]{2,1,0:T(8,128)S(1)}, f32[2,96,128]{2,1,0:T(8,128)S(1)}, u32[]{:S(2)}, u32[]{:S(2)}) %collective-permute-start.2) | collective-permute-done | bytes 98336 | tf_op jit(solution)/shard_map/ppermute | solution.py:294
  15.8 2.3 %collective-permute-start.4 = (f32[2,96,128]{2,1,0:T(8,128)S(1)}, f32[2,96,128]{2,1,0:T(8,128)S(1)}, u32[]{:S(2)}, u32[]{:S(2)}) collective-permute-start(f32[2,96,128]{2,1,0:T(8,128)S(1)} %broadcast_select_fusion), channel_id=1, source_target_pairs={{0,1},{1,0},{2,3},{3,2},{4,5},{5,4},{6,7},{7,6},{8,9},{9,8},{10,11... | collective-permute-start | bytes 294920 | tf_op jit(solution)/shard_map/ppermute | solution.py:294
  18.1 0.0 collective-permute-done.1.refs_1_
  18.1 0.9 %collective-permute-done.4.refs_4_ = f32[2,96,128]{2,1,0:T(8,128)S(1)} collective-permute-done((f32[2,96,128]{2,1,0:T(8,128)S(1)}, f32[2,96,128]{2,1,0:T(8,128)S(1)}, u32[]{:S(2)}, u32[]{:S(2)}) %collective-permute-start.4) | collective-permute-done | bytes 98336 | tf_op jit(solution)/shard_map/ppermute | solution.py:294
  19.0 0.0 copy-start
  19.0 1.1 %copy-done = bf16[4,368,240]{2,1,0:T(8,128)(2,1)S(1)} copy-done((bf16[4,368,240]{2,1,0:T(8,128)(2,1)S(1)}, bf16[4,368,240]{2,1,0:T(8,128)(2,1)}, u32[]{:S(2)}) %copy-start) | copy-done | bytes 706584
  20.2 0.0 copy-start.1
  20.2 1.1 %copy-done.1 = bf16[4,80,1104]{2,1,0:T(8,128)(2,1)S(1)} copy-done((bf16[4,80,1104]{2,1,0:T(8,128)(2,1)S(1)}, bf16[4,80,1104]{2,1,0:T(8,128)(2,1)}, u32[]{:S(2)}) %copy-start.1) | copy-done | bytes 706584
  21.3 0.0 copy-start.2
  21.3 0.9 %copy-done.2 = f32[272,128]{1,0:T(8,128)S(1)} copy-done((f32[272,128]{1,0:T(8,128)S(1)}, f32[272,128]{1,0:T(8,128)}, u32[]{:S(2)}) %copy-start.2) | copy-done | bytes 139288
  22.2 0.9 %copy-done.3 = bf16[256,256]{1,0:T(8,128)(2,1)S(1)} copy-done((bf16[256,256]{1,0:T(8,128)(2,1)S(1)}, bf16[256,256]{1,0:T(8,128)(2,1)}, u32[]{:S(2)}) %copy-start.3) | copy-done | bytes 131096
  23.1 0.9 %copy-done.4 = bf16[128,384]{1,0:T(8,128)(2,1)S(1)} copy-done((bf16[128,384]{1,0:T(8,128)(2,1)S(1)}, bf16[128,384]{1,0:T(8,128)(2,1)}, u32[]{:S(2)}) %copy-start.4) | copy-done | bytes 98328
  24.0 0.8 %copy-done.5 = f32[80,128]{1,0:T(8,128)S(1)} copy-done((f32[80,128]{1,0:T(8,128)S(1)}, f32[80,128]{1,0:T(8,128)}, u32[]{:S(2)}) %copy-start.5) | copy-done | bytes 40984
  24.8 16.8 %shard_map.109 = f32[96,128]{1,0:T(8,128)} custom-call(f32[8,256]{1,0:T(8,128)S(1)} %select_maximum_fusion.indices_ref, f32[2,96,128]{2,1,0:T(8,128)S(1)} %pad_maximum_fusion.refs_0_, f32[2,96,128]{2,1,0:T(8,128)S(1)} %collective-permute-done.1.refs_1_, f32[2,96,128]{2,1,0:T(8,128)S(1)} %collective-permute-done.2.refs_2_, ...), custom_call_target="tpu_custom_call" | custom-call | tf_op jit(solution)/shard_map/pallas_call | solution.py:333
  (9 shorter events, 0.0 us)
Async XLA Ops:
  2.3 3.6 %collective-permute-start = (f32[104,128]{1,0:T(8,128)S(1)}, f32[104,128]{1,0:T(8,128)S(1)}, u32[]{:S(2)}, u32[]{:S(2)}) collective-permute-start(f32[104,128]{1,0:T(8,128)S(1)} %maximum_maximum_fusion), channel_id=1, source_target_pairs={{0,16},{16,0},{1,17},{17,1},{2,18},{18,2},{3,19},{19,3},{4,20},{20... | collective-permute-start | bytes 159752 | tf_op jit(solution)/shard_map/ppermute | solution.py:300
  6.8 6.6 %collective-permute-start.3 = (f32[2,96,128]{2,1,0:T(8,128)S(1)}, f32[2,96,128]{2,1,0:T(8,128)S(1)}, u32[]{:S(2)}, u32[]{:S(2)}) collective-permute-start(f32[2,96,128]{2,1,0:T(8,128)S(1)} %pad_maximum_fusion.refs_0_), channel_id=1, source_target_pairs={{0,14},{1,15},{2,4},{3,5},{4,2},{5,3},{6,8},{7,9},{8,6},{9,7},{10,... | collective-permute-start | bytes 294920 | tf_op jit(solution)/shard_map/ppermute | solution.py:294
  11.3 4.5 %collective-permute-start.2 = (f32[2,96,128]{2,1,0:T(8,128)S(1)}, f32[2,96,128]{2,1,0:T(8,128)S(1)}, u32[]{:S(2)}, u32[]{:S(2)}) collective-permute-start(f32[2,96,128]{2,1,0:T(8,128)S(1)} %pad_maximum_fusion.refs_0_), channel_id=1, source_target_pairs={{0,2},{1,3},{2,0},{3,1},{4,6},{5,7},{6,4},{7,5},{8,10},{9,11},{10,... | collective-permute-start | bytes 294920 | tf_op jit(solution)/shard_map/ppermute | solution.py:294
  11.3 6.8 %collective-permute-start.1 = (f32[2,96,128]{2,1,0:T(8,128)S(1)}, f32[2,96,128]{2,1,0:T(8,128)S(1)}, u32[]{:S(2)}, u32[]{:S(2)}) collective-permute-start(f32[2,96,128]{2,1,0:T(8,128)S(1)} %pad_maximum_fusion.refs_0_), channel_id=1, source_target_pairs={{0,1},{1,0},{2,3},{3,2},{4,5},{5,4},{6,7},{7,6},{8,9},{9,8},{10,11... | collective-permute-start | bytes 294920 | tf_op jit(solution)/shard_map/ppermute | solution.py:294
  15.8 3.2 %collective-permute-start.4 = (f32[2,96,128]{2,1,0:T(8,128)S(1)}, f32[2,96,128]{2,1,0:T(8,128)S(1)}, u32[]{:S(2)}, u32[]{:S(2)}) collective-permute-start(f32[2,96,128]{2,1,0:T(8,128)S(1)} %broadcast_select_fusion), channel_id=1, source_target_pairs={{0,1},{1,0},{2,3},{3,2},{4,5},{5,4},{6,7},{7,6},{8,9},{9,8},{10,11... | collective-permute-start | bytes 294920 | tf_op jit(solution)/shard_map/ppermute | solution.py:294
  19.0 1.1 %copy-start = (bf16[4,368,240]{2,1,0:T(8,128)(2,1)S(1)}, bf16[4,368,240]{2,1,0:T(8,128)(2,1)}, u32[]{:S(2)}) copy-start(bf16[4,368,240]{2,1,0:T(8,128)(2,1)} %constant.26.clone.refs_5_) | copy-start | bytes 2119684
  20.2 1.1 %copy-start.1 = (bf16[4,80,1104]{2,1,0:T(8,128)(2,1)S(1)}, bf16[4,80,1104]{2,1,0:T(8,128)(2,1)}, u32[]{:S(2)}) copy-start(bf16[4,80,1104]{2,1,0:T(8,128)(2,1)} %constant.27.clone.refs_6_) | copy-start | bytes 2119684
  21.3 0.9 %copy-start.2 = (f32[272,128]{1,0:T(8,128)S(1)}, f32[272,128]{1,0:T(8,128)}, u32[]{:S(2)}) copy-start(f32[272,128]{1,0:T(8,128)} %constant.32.clone.refs_11_) | copy-start | bytes 417796
  22.2 0.9 %copy-start.3 = (bf16[256,256]{1,0:T(8,128)(2,1)S(1)}, bf16[256,256]{1,0:T(8,128)(2,1)}, u32[]{:S(2)}) copy-start(bf16[256,256]{1,0:T(8,128)(2,1)} %constant.31.clone.refs_10_) | copy-start | bytes 393220
  23.1 0.9 %copy-start.4 = (bf16[128,384]{1,0:T(8,128)(2,1)S(1)}, bf16[128,384]{1,0:T(8,128)(2,1)}, u32[]{:S(2)}) copy-start(bf16[128,384]{1,0:T(8,128)(2,1)} %constant.30.clone.refs_9_) | copy-start | bytes 294916
  24.0 0.8 %copy-start.5 = (f32[80,128]{1,0:T(8,128)S(1)}, f32[80,128]{1,0:T(8,128)}, u32[]{:S(2)}) copy-start(f32[80,128]{1,0:T(8,128)} %constant.33.clone.refs_12_) | copy-start | bytes 122884
where the time goes:
time: 42.3 us; the launch traced here: 41.6 us
  Pallas kernels  16.8 us (40%)
  starting transfers between devices  11 us (26%)
  local copies, waits for them, and re-layouts  5.8 us (14%)
  waiting for transfers between devices  4.87 us (12%)
  other arithmetic  2.39 us (6%)
  between operations  0.68 us (2%)
    pallas_call x1, Pallas kernels, exchange(): pl.pallas_call(functools.partial(exchange_kernel, batch, points, blocks),...  16.8 us
    ppermute x4, starting transfers between devices, swap(): lax.ppermute(value, axis, [(at, partner(at) % count) for at in range(coun...  8.9 us
    unnamed x12, local copies, waits for them, and re-layouts  5.72 us
    ppermute x4, waiting for transfers between devices, swap(): lax.ppermute(value, axis, [(at, partner(at) % count) for at in range(coun...  3.35 us
    ppermute x1, starting transfers between devices, rest_of_ring(): lax.ppermute(value, axis, [(at, (at + step) % count) for at in range(coun...  2.11 us
    ppermute x1, waiting for transfers between devices, rest_of_ring(): lax.ppermute(value, axis, [(at, (at + step) % count) for at in range(coun...  1.52 us
    concatenate x1, other arithmetic, shards(): jnp.concatenate([own, indices, jnp.zeros((6, per_owner), jnp.float32)], a...  0.87 us
  transfers between devices with their start and end apart: 5, of which 3 were waited for; matrix products, arithmetic and copies ran while one was open for 0% of the time, Pallas kernels for 0%

commit v1 on v0

--- a/solution.py
+++ b/solution.py
@@ -15,6 +15,7 @@
 screen_width = 16.0
 LANES = 128
 ROWS = 16
+SMALL = 512
 
 
 def round_up(value, unit):
@@ -71,13 +72,11 @@
     n_picked = round_up(len(picked), ROWS)
 
     def stack(tables, rows, cols):
-        head = np.zeros((4, rows, 3 * cols), ml_dtypes.bfloat16)
+        full = np.zeros((4, rows, cols))
         for at, table in enumerate(tables):
-            full = np.zeros((rows, cols))
-            full[: table.shape[0], : table.shape[1]] = table
-            high, low = split_table(full)
-            head[at] = np.concatenate([high, high, low], axis=1)
-        return head
+            full[at, : table.shape[0], : table.shape[1]] = table
+        high, low = split_table(full)
+        return np.concatenate([high, high, low], axis=2)
 
     scale = points**-1.5
     small = class_waves(picked)
@@ -110,13 +109,13 @@
     double = np.where(2 * freqs % grid == 0, 1.0, 2.0)
     kernel = kernel * (double[:, 0] * double[:, 1])[:, None]
     kernel = kernel * (points / grid) ** 2 / float(points**3)
-    weights = np.zeros((n_pairs, lanes), np.float32)
+    weights = np.zeros((n_pairs, lanes))
     for member in range(members):
         weights[: len(pairs), member * points : (member + 1) * points] = kernel
 
-    codes = np.full((n_picked, LANES), -7.0, np.float32)
+    codes = np.full((n_picked, LANES), -7.0)
     for at, (b, c) in enumerate(picked):
-        codes[at] = b * points + c
+        codes[at, 0], codes[at, 1] = b, c
     return dict(
         synth=synth,
         project=project,
@@ -124,9 +123,42 @@
         inverse=inverse,
         turn_left=turn_left,
         turn_right=turn_right,
-        weights=weights,
-        codes=codes,
+        weights=np.concatenate(split_table(weights), axis=1),
+        codes=codes.astype(ml_dtypes.bfloat16),
     )
+
+
+def pack_tables(tables):
+    shelves = (("forward",), ("project",), ("inverse", "synth"))
+    shelves += (("turn_left", "turn_right", "weights", "codes"),)
+    flat = {name: table.reshape(-1, table.shape[-1]) for name, table in tables.items()}
+    where, row, width = {}, 0, 0
+    for shelf in shelves:
+        column = 0
+        for name in shelf:
+            where[name] = (row, column)
+            column += round_up(flat[name].shape[1], LANES)
+        row += round_up(max(flat[name].shape[0] for name in shelf), ROWS)
+        width = max(width, column)
+    packed = np.zeros((row, width), ml_dtypes.bfloat16)
+    for name, (first, column) in where.items():
+        rows, cols = flat[name].shape
+        packed[first : first + rows, column : column + cols] = flat[name]
+    return packed, where
+
+
+def table_getter(shapes, refs, where):
+    def get(name, at=None):
+        shape = shapes[name]
+        if where is None:
+            ref = refs[TABLE_NAMES.index(name)]
+            return ref[...] if at is None else ref[at]
+        first, column = where[name]
+        rows = shape[-2]
+        first = first if at is None else first + at * rows
+        return refs[0][first : first + rows, column : column + shape[-1]]
+
+    return get
 
 
 TABLE_NAMES = (
@@ -156,14 +188,17 @@
     return jnp.concatenate([high, low, high], axis=0)
 
 
+def product(table, value):
+    return dot(table, stacked(value))
+
+
 def pick_matrix(indices, codes, points):
     first, second = indices[0:1], indices[1:2]
     alive = first >= 0.0
     signed_first = jnp.where(first < points // 2, first, first - points)
     signed_second = jnp.where(second < points // 2, second, second - points)
-    code = jnp.abs(signed_first) * points + jnp.abs(signed_second)
-    code = jnp.where(alive, code, -1.0)
-    one = jnp.where(codes[:, 0:1] == code, 1.0, 0.0)
+    first_same = codes[:, 0:1] == jnp.where(alive, jnp.abs(signed_first), -1.0)
+    one = jnp.where(first_same & (codes[:, 1:2] == jnp.abs(signed_second)), 1.0, 0.0)
     sign_first = jnp.where(signed_first < 0.0, -1.0, 1.0)
     sign_second = jnp.where(signed_second < 0.0, -1.0, 1.0)
     parts = [one, one * sign_first, one * sign_second, one * (sign_first * sign_second)]
@@ -194,7 +229,8 @@
         pl.loop(0, 4)(body)
 
 
-def synthesize(small, blocks, pick, turn_left, synth_ref, coefs_ref, orbs_ref):
+def synthesize(small, blocks, pick, get, coefs_ref, orbs_ref):
+    turn_left = get("turn_left")
     fields = [dot(turn_left, stacked(block)) for block in blocks]
     field = fields[0] if len(fields) == 1 else jnp.concatenate(fields, axis=0)
     high, low = split(field)
@@ -206,31 +242,39 @@
         coefs_ref[at] = coefs[at * rows : (at + 1) * rows]
 
     def body(at):
-        orbs_ref[at] = dot(synth_ref[at], stacked(coefs_ref[at]))
+        orbs_ref[at] = product(get("synth", at), coefs_ref[at])
 
     each_part(small, body)
     for at, quadrant in enumerate(unfold([orbs_ref[at] for at in range(4)])):
         orbs_ref[at] = quadrant
 
 
-def exchange_kernel(
-    members,
-    points,
-    group_blocks,
-    indices_ref,
-    *refs,
-):
-    count = sum(group_blocks)
-    coef_refs = refs[:count]
-    tables = refs[count : count + len(TABLE_NAMES)]
-    synth_ref, project_ref, forward_ref, inverse_ref = tables[:4]
-    turn_left_ref, turn_right_ref, weights_ref, codes_ref = tables[4:]
-    out_ref, own_ref, visit_ref, field_ref, work_ref, coefs_ref = refs[count + len(TABLE_NAMES) :]
-    pick = pick_matrix(indices_ref[...], codes_ref[...], points)
-    turn_left, turn_right = turn_left_ref[...], turn_right_ref[...]
+def exchange_kernel(members, points, sizes, begins, ends, shapes, where, *refs):
+    refs = list(refs)
+    take = lambda count: [refs.pop(0) for _ in range(count)]
+    prior_ref = None
+    if begins:
+        indices_ref, flag_in_ref = take(2)
+    else:
+        pick_ref, own_ref, prior_ref = take(3)
+    coef_refs = take(sum(sizes))
+    get = table_getter(shapes, take(len(TABLE_NAMES) if where is None else 1), where)
+    if ends:
+        (out_ref,) = take(1)
+    elif begins:
+        pick_ref, own_ref, field_ref, flag_ref = take(4)
+        flag_ref[...] = flag_in_ref[...]
+    else:
+        (field_ref,) = take(1)
+    visit_all_ref, work_all_ref, coefs_all_ref = take(3)
+    if begins and ends:
+        pick_ref, own_ref, field_ref = take(3)
+    if begins:
+        pick_ref[...] = pick_matrix(indices_ref[...], get("codes").astype(jnp.float32), points)
+    pick, turn_right = pick_ref[...], get("turn_right")
     lanes = turn_right.shape[0] // 2
     pad = lanes - members * points
-    small = forward_ref.shape[1] <= 512
+    small = where is not None
 
     def coefs_of(ref):
         block = jnp.concatenate([ref[at] for at in range(ref.shape[0])], axis=1)
@@ -238,55 +282,88 @@
             block = jnp.concatenate([block, jnp.zeros((pad, block.shape[1]), block.dtype)], axis=0)
         return block
 
-    synthesize(
-        small,
-        [coefs_of(coef_refs[0])],
-        pick,
-        turn_left,
-        synth_ref,
-        coefs_ref.at[:, :, :lanes],
-        own_ref,
-    )
-    field_ref[...] = jnp.zeros_like(field_ref)
+    weight = get("weights").astype(jnp.float32)
+    weight = weight[:, :lanes] + weight[:, lanes:]
     start = 0
-    for size in group_blocks:
+    for step, size in enumerate(sizes):
+        refs = [ref.at[:, :, : size * lanes] for ref in (visit_all_ref, work_all_ref, coefs_all_ref)]
+        visit_ref, work_ref, coefs_ref = refs
         blocks = [coefs_of(ref) for ref in coef_refs[start : start + size]]
         start += size
-        wide = size * lanes
-        visit, work = visit_ref.at[:, :, :wide], work_ref.at[:, :, :wide]
-        synthesize(small, blocks, pick, turn_left, synth_ref, coefs_ref.at[:, :, :wide], visit)
-
+        synthesize(small, blocks, pick, get, coefs_ref, visit_ref)
+        if begins and step == 0:
+            for at in range(4):
+                own_ref[at] = visit_ref[at, :, :lanes]
+        weights = jnp.concatenate([weight] * size, axis=1)
         density = []
         for at in range(4):
-            own = own_ref[at]
-            both = own if size == 1 else jnp.concatenate([own] * size, axis=1)
-            density.append(both * visit[at])
-        for at, part in enumerate(unfold(density)):
-            work[at] = part
-
-        def poisson(at):
-            spectrum = dot(forward_ref[at], stacked(work[at]))
-            spectrum = turn(spectrum, turn_right)
-            weights = weights_ref[...]
-            weights = weights if size == 1 else jnp.concatenate([weights] * size, axis=1)
-            spectrum = turn(spectrum * weights, turn_right)
-            work[at] = dot(inverse_ref[at], stacked(spectrum))
-
-        each_part(small, poisson)
-        for at, quadrant in enumerate(unfold([work[at] for at in range(4)])):
-            term = quadrant * visit[at]
+            density.append(jnp.concatenate([own_ref[at]] * size, axis=1) * visit_ref[at])
+        density = unfold(density)
+        if small:
+            spectra = [product(get("forward", at), density[at]) for at in range(4)]
+            spectrum = turn(jnp.concatenate(spectra, axis=0), turn_right)
+            spectrum = turn(spectrum * jnp.concatenate([weights] * 4, axis=0), turn_right)
+            rows = weights.shape[0]
+            potential = [
+                product(get("inverse", at), spectrum[at * rows : (at + 1) * rows]) for at in range(4)
+            ]
+        else:
+            for at, part in enumerate(density):
+                work_ref[at] = part
+
+            @pl.loop(0, 4)
+            def poisson(at):
+                spectrum = turn(product(get("forward", at), work_ref[at]), turn_right)
+                spectrum = turn(spectrum * weights, turn_right)
+                work_ref[at] = product(get("inverse", at), spectrum)
+
+            potential = [work_ref[at] for at in range(4)]
+        field = []
+        for at, quadrant in enumerate(unfold(potential)):
+            term = quadrant * visit_ref[at]
             total = term[:, :lanes]
             for block in range(1, size):
                 total = total + term[:, block * lanes : (block + 1) * lanes]
-            field_ref[at] += total
-
-    field = unfold([field_ref[at] for at in range(4)])
-    coefs = [dot(project_ref[at], stacked(field[at])) for at in range(4)]
-    coefs = turn(jnp.concatenate(coefs, axis=0), turn_right)
-    high, low = split(coefs.T)
-    own_pick = pick[:, : out_ref.shape[1]]
-    result = dot(high, own_pick) + dot(low, own_pick)
-    out_ref[...] = result[: members * points]
+            if prior_ref is not None:
+                total = total + prior_ref[at]
+            if ends and step == len(sizes) - 1:
+                field.append(total)
+            else:
+                field_ref[at] = total
+        if not (ends and step == len(sizes) - 1):
+            prior_ref = field_ref
+    if ends:
+        field = unfold(field)
+        coefs = [product(get("project", at), field[at]) for at in range(4)]
+        coefs = turn(jnp.concatenate(coefs, axis=0), turn_right)
+        high, low = split(coefs.T)
+        own_pick = pick[:, : out_ref.shape[1]]
+        result = dot(high, own_pick) + dot(low, own_pick)
+        out_ref[...] = result[: members * points]
+
+
+def load_kernel(*refs):
+    semaphores = refs[-1]
+    count = (len(refs) - 1) // 2
+    copies = [
+        pltpu.make_async_copy(refs[at], refs[count + at], semaphores.at[at]) for at in range(count)
+    ]
+    for copy in copies:
+        copy.start()
+    for copy in copies:
+        copy.wait()
+
+
+def load(values):
+    return pl.pallas_call(
+        load_kernel,
+        out_shape=[jax.ShapeDtypeStruct(value.shape, value.dtype) for value in values],
+        in_specs=[pl.BlockSpec(memory_space=pl.ANY)] * len(values),
+        out_specs=[pl.BlockSpec(memory_space=pltpu.VMEM)] * len(values),
+        scratch_shapes=[pltpu.SemaphoreType.DMA((len(values),))],
+        cost_estimate=pl.CostEstimate(flops=0, bytes_accessed=2**20, transcendentals=0),
+        compiler_params=pltpu.CompilerParams(vmem_limit_bytes=16 * 2**20),
+    )(*values)
 
 
 def swap(value, axis, partner):
@@ -307,50 +384,81 @@
     owners = lax.axis_size("pw")
     batch = max(n for n in range(1, members + 1) if members % n == 0 and (n == 1 or n * points <= LANES))
     tables = build_tables(points, per_owner * owners, batch)
+    shapes = {name: table.shape for name, table in tables.items()}
+    small = tables["inverse"].shape[1] <= SMALL
+    where = None
+    if small:
+        packed, where = pack_tables(tables)
+        values = [jnp.asarray(packed)]
+    else:
+        values = [jnp.asarray(tables[name]) for name in TABLE_NAMES]
+    own = stick_coefs.reshape(members * points, per_owner)
+    others = rest_of_ring(own, "pw")
+    if batch == members:
+        (own,) = load([own])
     position = jnp.arange(per_owner, dtype=jnp.int32)[None]
     indices = jnp.where(position < stick_count[0], miller, -1).astype(jnp.float32)
-    own = stick_coefs.reshape(members * points, per_owner)
-    load = jnp.concatenate([own, indices, jnp.zeros((6, per_owner), jnp.float32)], axis=0)
-    loads = [load] + rest_of_ring(load, "pw")
-    coefs = jnp.stack([part[: members * points] for part in loads])
-    indices = jnp.concatenate([part[members * points :] for part in loads], axis=1)
+    indices = jnp.concatenate([indices, jnp.zeros((6, per_owner), jnp.float32)], axis=0)
+    indices = jnp.concatenate([indices] + rest_of_ring(indices, "pw"), axis=1)
 
     ring = lax.axis_size("band")
+    coefs = jnp.stack([own] + others)
     mate = swap(coefs, "band", lambda at: at ^ 1)
-    near = swap(coefs, "band", lambda at: at ^ 2)
-    far = swap(coefs, "band", lambda at: at + 2 if at & 2 else at - 2 + ring)
-    me = lax.axis_index("band")
-    near_goes = (me & 1) == ((me >> 1) & 1)
-    last = swap(jnp.where(near_goes, near, far), "band", lambda at: at ^ 1)
+    got = swap(jnp.stack([coefs, mate]), "band", lambda at: at + 1 if at & 1 else at - 1 + ring)
 
     lanes = tables["turn_right"].shape[0] // 2
     n_place, n_picked = tables["synth"].shape[1], tables["project"].shape[1]
-    blocks = (2, 2, 1)
     vmem = pl.BlockSpec(memory_space=pltpu.VMEM)
-    values = [jnp.asarray(tables[name]) for name in TABLE_NAMES]
-
-    def exchange(pieces):
+    grid_shape = jax.ShapeDtypeStruct((4, n_place, lanes), jnp.float32)
+
+    pick_shape = jax.ShapeDtypeStruct((4 * n_picked, per_owner * owners), jnp.bfloat16)
+    out_shape = jax.ShapeDtypeStruct((batch * points, per_owner), jnp.float32)
+
+    def call(sizes, carried, groups_in, out_shape, begins=False, ends=False):
+        wide = max(sizes) * lanes
+        scratch = [
+            pltpu.VMEM((4, n_place, wide), jnp.float32),
+            pltpu.VMEM((4, 8 if small else n_place, wide), jnp.float32),
+            pltpu.VMEM((4, n_picked, wide), jnp.float32),
+        ]
+        if begins and ends:
+            scratch += [pltpu.VMEM(each.shape, each.dtype) for each in (pick_shape, grid_shape, grid_shape)]
         return pl.pallas_call(
-            functools.partial(exchange_kernel, batch, points, blocks),
-            out_shape=jax.ShapeDtypeStruct((batch * points, per_owner), jnp.float32),
-            in_specs=[vmem] * (1 + len(pieces) + len(values)),
-            out_specs=vmem,
-            scratch_shapes=[
-                pltpu.VMEM((4, n_place, lanes), jnp.float32),
-                pltpu.VMEM((4, n_place, 2 * lanes), jnp.float32),
-                pltpu.VMEM((4, n_place, lanes), jnp.float32),
-                pltpu.VMEM((4, n_place, 2 * lanes), jnp.float32),
-                pltpu.VMEM((4, n_picked, 2 * lanes), jnp.float32),
-            ],
-            compiler_params=pltpu.CompilerParams(vmem_limit_bytes=50 * 2**20),
-        )(indices, *pieces, *values)
-
-    pieces = (coefs, mate, near, far, last)
-    if batch == members:
-        result = exchange(pieces)
+            functools.partial(exchange_kernel, batch, points, sizes, begins, ends, shapes, where),
+            out_shape=out_shape,
+            in_specs=[vmem] * (len(carried) + len(groups_in) + len(values)),
+            out_specs=jax.tree.map(lambda _: vmem, out_shape),
+            scratch_shapes=scratch,
+            cost_estimate=pl.CostEstimate(flops=5 * 10**9, bytes_accessed=4 * 2**20, transcendentals=0),
+            compiler_params=pltpu.CompilerParams(vmem_limit_bytes=(24 if small else 50) * 2**20),
+        )(*carried, *groups_in, *values)
+
+    flag = jnp.ones((batch * points, per_owner), jnp.float32)
+    if small and batch == members:
+        pick, orbs, field, flag = call(
+            (2,),
+            (indices, flag),
+            (coefs, mate),
+            (pick_shape, grid_shape, grid_shape, jax.ShapeDtypeStruct(flag.shape, flag.dtype)),
+            begins=True,
+        )
+        last = swap(jnp.where(flag > 0.0, got[0], 0.0), "band", lambda at: at ^ 1)
+        field = call((2,), (pick, orbs, field), (got[0], got[1]), grid_shape)
+        result = call((1,), (pick, orbs, field), (last,), out_shape, ends=True)
     else:
-        cut = lambda piece: piece.reshape(owners, -1, batch * points, per_owner).swapaxes(0, 1)
-        result = lax.map(exchange, tuple(cut(piece) for piece in pieces))
+        last = swap(got[0], "band", lambda at: at ^ 1)
+
+        def exchange(pieces):
+            return call((2, 2, 1), (indices, flag), pieces, out_shape, begins=True, ends=True)
+
+        def cut(piece):
+            return piece.reshape(owners, -1, batch * points, per_owner).swapaxes(0, 1)
+
+        pieces = (coefs, mate, got[0], got[1], last)
+        if batch == members:
+            result = exchange(pieces)
+        else:
+            result = lax.map(exchange, tuple(cut(piece) for piece in pieces))
     return result.reshape(groups, members, points, per_owner)
 
 

time: 42.3 us -> 26.6 us (0.63); the launches traced: 41.6 us -> 26.3 us
  Pallas kernels: 16.8 us -> 11.5 us
  waiting for transfers between devices: 4.87 us -> 0.95 us
  starting transfers between devices: 11 us -> 8.44 us
  local copies, waits for them, and re-layouts: 5.8 us -> 3.88 us
  other arithmetic: 2.39 us -> 0.75 us
    pallas_call x1 -> x4, Pallas kernels: 16.8 us -> 11.5 us  [the longest x3 11.5 us: call(): pl.pallas_call(functools.partial(exchange_kernel, batch, points, sizes, b...]
    ppermute x4 -> x3, waiting for transfers between devices: 3.35 us -> 0.45 us  [swap(): lax.ppermute(value, axis, [(at, partner(at) % count) for at in range(coun...]
    ppermute x4 -> x3, starting transfers between devices: 8.9 us -> 6.4 us  [swap(): lax.ppermute(value, axis, [(at, partner(at) % count) for at in range(coun...]
    unnamed x12 -> x6, local copies, waits for them, and re-layouts: 5.72 us -> 3.86 us
    ppermute x1 -> x2, waiting for transfers between devices: 1.52 us -> 0.5 us  [rest_of_ring(): lax.ppermute(value, axis, [(at, (at + step) % count) for at in range(coun...]
    concatenate x2 -> x1, other arithmetic: 0.88 us -> 0.01 us  [shards(): indices = jnp.concatenate([indices] + rest_of_ring(indices, 'pw'), axis=1)]
    another operation x1 -> x2, other arithmetic: 0.81 us -> 0.04 us  [shards(): jnp.stack([coefs, mate])]
    ppermute x1 -> x2, starting transfers between devices: 2.11 us -> 2.04 us  [rest_of_ring(): lax.ppermute(value, axis, [(at, (at + step) % count) for at in range(coun...]
  transfers between devices with their start and end apart: 5 -> 5, of which waited for: 3 -> 2; matrix products, arithmetic and copies ran while one was open for 0% -> 3% of each run, Pallas kernels for 0% -> 27%
where the time goes in v1:
time: 26.6 us; the launch traced here: 26.3 us
  Pallas kernels  11.5 us (43%)
  starting transfers between devices  8.44 us (32%)
  local copies, waits for them, and re-layouts  3.88 us (15%)
  waiting for transfers between devices  0.95 us (4%)
  other arithmetic  0.75 us (3%)
  between operations  0.75 us (3%)
    pallas_call x3, Pallas kernels, call(): pl.pallas_call(functools.partial(exchange_kernel, batch, points, sizes, b...  11.5 us
    ppermute x3, starting transfers between devices, swap(): lax.ppermute(value, axis, [(at, partner(at) % count) for at in range(coun...  6.4 us
    unnamed x6, local copies, waits for them, and re-layouts  3.86 us
    ppermute x2, starting transfers between devices, rest_of_ring(): lax.ppermute(value, axis, [(at, (at + step) % count) for at in range(coun...  2.04 us
    convert_element_type x1, other arithmetic, shards(): jnp.where(position < stick_count[0], miller, -1).astype(jnp.float32)  0.69 us
  transfers between devices with their start and end apart: 5, of which 2 were waited for; matrix products, arithmetic and copies ran while one was open for 3% of the time, Pallas kernels for 27%

profile of v1, /device:TPU:1, one launch (start us, length us, event | category | flops | bytes accessed | tf_op | source)
XLA Modules:
  0.0 26.3 jit_solution(13929269839408425717)
XLA Ops:
  0.0 2.0 %collective-permute-start.1 = (f32[96,128]{1,0:T(8,128)}, f32[96,128]{1,0:T(8,128)S(1)}, u32[]{:S(2)}, u32[]{:S(2)}) collective-permute-start(f32[96,128]{1,0:T(8,128)} %bitcast.17), channel_id=1, source_target_pairs={{0,16},{16,0},{1,17},{17,1},{2,18},{18,2},{3,19},{19,3},{4,20},{20... | collective-permute-start | bytes 147464 | tf_op jit(solution)/shard_map/ppermute | solution.py:377
  2.7 0.7 %select_convert_fusion = f32[2,128]{1,0:T(2,128)S(1)} fusion(s32[2,128]{1,0:T(2,128)} %param.5, pred[128]{0:T(512)(128)(4,1)S(1)} %iota_compare_fusion), kind=kLoop, calls=%fused_computation.7 | loop fusion | flops 512 | bytes 2176 | tf_op jit(solution)/shard_map/convert_element_type | solution.py:400
  3.4 0.0 collective-permute-start
  3.4 0.0 copy-start
  3.4 0.8 %copy-done = f32[1,2,48,128]{3,2,1,0:T(8,128)S(1)} copy-done((f32[1,2,48,128]{3,2,1,0:T(8,128)S(1)}, f32[1,2,48,128]{3,2,1,0:T(8,128)}, u32[]{:S(2)}) %copy-start) | copy-done | bytes 49176
  4.3 0.0 collective-permute-done.1
  4.3 1.1 %collective-permute-start.2 = (f32[2,96,128]{2,1,0:T(8,128)S(1)}, f32[2,96,128]{2,1,0:T(8,128)S(1)}, u32[]{:S(2)}, u32[]{:S(2)}) collective-permute-start(f32[2,96,128]{2,1,0:T(8,128)S(1)} %get-tuple-element.16.refs_2_), channel_id=1, source_target_pairs={{0,1},{1,0},{2,3},{3,2},{4,5},{5,4},{6,7},{7,6},{8,9},{9,8},{10,11... | collective-permute-start | bytes 294920 | tf_op jit(solution)/shard_map/ppermute | solution.py:371
  5.4 0.5 %collective-permute-done = f32[8,128]{1,0:T(8,128)S(1)} collective-permute-done((f32[8,128]{1,0:T(8,128)S(1)}, f32[8,128]{1,0:T(8,128)S(1)}, u32[]{:S(2)}, u32[]{:S(2)}) %collective-permute-start) | collective-permute-done | bytes 4128 | tf_op jit(solution)/shard_map/ppermute | solution.py:377
  5.9 0.4 %collective-permute-done.2.refs_3_ = f32[2,96,128]{2,1,0:T(8,128)S(1)} collective-permute-done((f32[2,96,128]{2,1,0:T(8,128)S(1)}, f32[2,96,128]{2,1,0:T(8,128)S(1)}, u32[]{:S(2)}, u32[]{:S(2)}) %collective-permute-start.2) | collective-permute-done | bytes 98336 | tf_op jit(solution)/shard_map/ppermute | solution.py:371
  6.3 2.9 %collective-permute-start.3 = (f32[2,2,96,128]{3,2,1,0:T(8,128)S(1)}, f32[2,2,96,128]{3,2,1,0:T(8,128)S(1)}, u32[]{:S(2)}, u32[]{:S(2)}) collective-permute-start(f32[2,2,96,128]{3,2,1,0:T(8,128)S(1)} %pad_maximum_fusion), channel_id=1, source_target_pairs={{0,15},{1,2},{2,1},{3,4},{4,3},{5,6},{6,5},{7,8},{8,7},{9,10},{10,... | collective-permute-start | bytes 589832 | tf_op jit(solution)/shard_map/ppermute | solution.py:371
  9.2 0.0 copy-start.1
  9.2 3.1 %copy-done.1 = bf16[3152,1152]{1,0:T(8,128)(2,1)S(1)} copy-done((bf16[3152,1152]{1,0:T(8,128)(2,1)S(1)}, bf16[3152,1152]{1,0:T(8,128)(2,1)}, u32[]{:S(2)}) %copy-start.1) | copy-done | bytes 7262232
  12.2 0.0 copy-start.2
  12.2 3.5 %shard_map.47 = (bf16[320,256]{1,0:T(8,128)(2,1)S(1)}, f32[4,368,128]{2,1,0:T(8,128)S(1)}, f32[4,368,128]{2,1,0:T(8,128)S(1)}, f32[96,128]{1,0:T(8,128)S(1)}) custom-call(f32[8,256]{1,0:T(8,128)S(1)} %pad_maximum_fusion.2.refs_0_, f32[96,128]{1,0:T(8,128)S(1)} %broadcast_in_dim.27.refs_1_, f32[2,96,128]{2,1,0:T(8,128)S(1)} %get-tuple-element.16.refs_2_, ...), custom_call_target="tpu_custom_call" | custom-call | flops 5000000000 | bytes 4194304 | tf_op jit(solution)/shard_map/pallas_call | solution.py:426
  15.8 0.0 collective-permute-done.3
  15.8 2.5 %collective-permute-start.4 = (f32[2,96,128]{2,1,0:T(8,128)S(1)}, f32[2,96,128]{2,1,0:T(8,128)S(1)}, u32[]{:S(2)}, u32[]{:S(2)}) collective-permute-start(f32[2,96,128]{2,1,0:T(8,128)S(1)} %broadcast_select_fusion), channel_id=1, source_target_pairs={{0,1},{1,0},{2,3},{3,2},{4,5},{5,4},{6,7},{7,6},{8,9},{9,8},{10,11... | collective-permute-start | bytes 294920 | tf_op jit(solution)/shard_map/ppermute | solution.py:371
  18.3 0.0 copy-done.2
  18.3 3.5 %shard_map.48.refs_2_ = f32[4,368,128]{2,1,0:T(8,128)S(1)} custom-call(bf16[320,256]{1,0:T(8,128)(2,1)S(1)} %get-tuple-element.9.refs_0_, f32[4,368,128]{2,1,0:T(8,128)S(1)} %get-tuple-element.10.refs_1_, f32[4,368,128]{2,1,0:T(8,128)S(1)} %get-tuple-element.11.refs_2_, f32[2,96,128]{2,1,0:T(8,128)S(1)} %get-tuple-element.14.refs_3_, ...), custom_call_target="tpu_custom_call" | custom-call | flops 5000000000 | bytes 4194304 | tf_op jit(solution)/shard_map/pallas_call | solution.py:426
  21.9 0.0 collective-permute-done.4.refs_3_
  21.9 4.5 %shard_map.49 = f32[96,128]{1,0:T(8,128)} custom-call(bf16[320,256]{1,0:T(8,128)(2,1)S(1)} %get-tuple-element.9.refs_0_, f32[4,368,128]{2,1,0:T(8,128)S(1)} %get-tuple-element.10.refs_1_, f32[4,368,128]{2,1,0:T(8,128)S(1)} %shard_map.48.refs_2_, f32[2,96,128]{2,1,0:T(8,128)S(1)} %collective-permute-done.4.refs_3_, bf16[3152,1152]{1,0:T(8,128)(2,1)S(1)} %copy-done.2), custom_call_target="tpu_custom_call" | custom-call | flops 5000000000 | bytes 4194304 | tf_op jit(solution)/shard_map/pallas_call | solution.py:426
  (10 shorter events, 0.1 us)
Async XLA Ops:
  0.0 4.3 %collective-permute-start.1 = (f32[96,128]{1,0:T(8,128)}, f32[96,128]{1,0:T(8,128)S(1)}, u32[]{:S(2)}, u32[]{:S(2)}) collective-permute-start(f32[96,128]{1,0:T(8,128)} %bitcast.17), channel_id=1, source_target_pairs={{0,16},{16,0},{1,17},{17,1},{2,18},{18,2},{3,19},{19,3},{4,20},{20... | collective-permute-start | bytes 147464 | tf_op jit(solution)/shard_map/ppermute | solution.py:377
  3.4 2.5 %collective-permute-start = (f32[8,128]{1,0:T(8,128)S(1)}, f32[8,128]{1,0:T(8,128)S(1)}, u32[]{:S(2)}, u32[]{:S(2)}) collective-permute-start(f32[8,128]{1,0:T(8,128)S(1)} %concatenate.6), channel_id=1, source_target_pairs={{0,16},{16,0},{1,17},{17,1},{2,18},{18,2},{3,19},{19,3},{4,20},{20... | collective-permute-start | bytes 12296 | tf_op jit(solution)/shard_map/ppermute | solution.py:377
  3.4 0.8 %copy-start = (f32[1,2,48,128]{3,2,1,0:T(8,128)S(1)}, f32[1,2,48,128]{3,2,1,0:T(8,128)}, u32[]{:S(2)}) copy-start(f32[1,2,48,128]{3,2,1,0:T(8,128)} %param.4) | copy-start | bytes 147460
  4.3 2.0 %collective-permute-start.2 = (f32[2,96,128]{2,1,0:T(8,128)S(1)}, f32[2,96,128]{2,1,0:T(8,128)S(1)}, u32[]{:S(2)}, u32[]{:S(2)}) collective-permute-start(f32[2,96,128]{2,1,0:T(8,128)S(1)} %get-tuple-element.16.refs_2_), channel_id=1, source_target_pairs={{0,1},{1,0},{2,3},{3,2},{4,5},{5,4},{6,7},{7,6},{8,9},{9,8},{10,11... | collective-permute-start | bytes 294920 | tf_op jit(solution)/shard_map/ppermute | solution.py:371
  6.3 9.5 %collective-permute-start.3 = (f32[2,2,96,128]{3,2,1,0:T(8,128)S(1)}, f32[2,2,96,128]{3,2,1,0:T(8,128)S(1)}, u32[]{:S(2)}, u32[]{:S(2)}) collective-permute-start(f32[2,2,96,128]{3,2,1,0:T(8,128)S(1)} %pad_maximum_fusion), channel_id=1, source_target_pairs={{0,15},{1,2},{2,1},{3,4},{4,3},{5,6},{6,5},{7,8},{8,7},{9,10},{10,... | collective-permute-start | bytes 589832 | tf_op jit(solution)/shard_map/ppermute | solution.py:371
  9.2 3.1 %copy-start.1 = (bf16[3152,1152]{1,0:T(8,128)(2,1)S(1)}, bf16[3152,1152]{1,0:T(8,128)(2,1)}, u32[]{:S(2)}) copy-start(bf16[3152,1152]{1,0:T(8,128)(2,1)} %constant.2.clone.refs_4_.refs_5_) | copy-start | bytes 21786628
  12.2 6.1 %copy-start.2 = (bf16[3152,1152]{1,0:T(8,128)(2,1)S(1)}, bf16[3152,1152]{1,0:T(8,128)(2,1)}, u32[]{:S(2)}) copy-start(bf16[3152,1152]{1,0:T(8,128)(2,1)} %constant.2.clone.refs_4_.refs_5_) | copy-start | bytes 21786628
  15.8 6.0 %collective-permute-start.4 = (f32[2,96,128]{2,1,0:T(8,128)S(1)}, f32[2,96,128]{2,1,0:T(8,128)S(1)}, u32[]{:S(2)}, u32[]{:S(2)}) collective-permute-start(f32[2,96,128]{2,1,0:T(8,128)S(1)} %broadcast_select_fusion), channel_id=1, source_target_pairs={{0,1},{1,0},{2,3},{3,2},{4,5},{5,4},{6,7},{7,6},{8,9},{9,8},{10,11... | collective-permute-start | bytes 294920 | tf_op jit(solution)/shard_map/ppermute | solution.py:371

commit v2 on v1

--- a/solution.py
+++ b/solution.py
@@ -16,6 +16,7 @@
 LANES = 128
 ROWS = 16
 SMALL = 512
+PARITIES = ("cc", "sc", "cs", "ss")
 
 
 def round_up(value, unit):
@@ -48,45 +49,58 @@
             for b in {fold(b1 + b2), fold(b1 - b2)}:
                 for c in {fold(c1 + c2), fold(c1 - c2)}:
                     pairs.add((b, c))
-    pairs = sorted(pairs)
     near = grid // 2 + 1
-    place = [(y, z) for y in range(near) for z in range(near)]
-    once = np.array([0.5 if 2 * y % grid == 0 else 1.0 for y in range(near)])
-    place_weight = np.array([once[y] * once[z] for y, z in place])
+
+    def mirrored(value):
+        return 2 * value % grid != 0
+
+    def order(spots):
+        return sorted(spots, key=lambda spot: (not mirrored(spot[0]), not mirrored(spot[1]), spot))
+
+    pairs = order(pairs)
+    place = order((y, z) for y in range(near) for z in range(near))
+    place_weight = np.array([np.prod([1.0 if mirrored(v) else 0.5 for v in spot]) for spot in place])
+    small = len(place) <= SMALL
 
     def wave(kind, freq, spot):
         angle = 2.0 * np.pi * ((freq[:, None] * spot[None, :]) % grid) / grid
         return np.cos(angle) if kind == "c" else np.sin(angle)
 
-    spots = np.array(place)
-
-    def class_waves(freqs):
-        freqs = np.array(freqs)
-        return [
-            wave(ky, freqs[:, 0], spots[:, 0]) * wave(kz, freqs[:, 1], spots[:, 1])
-            for ky, kz in ("cc", "sc", "cs", "ss")
-        ]
+    def class_waves(kinds, freqs):
+        freqs, spots = np.array(freqs), np.array(place)
+        first = wave(kinds[0], freqs[:, 0], spots[:, 0])
+        return first * wave(kinds[1], freqs[:, 1], spots[:, 1])
+
+    def class_pairs(kinds):
+        if not small:
+            return pairs
+        if kinds == "cs":
+            return [(c, b) for b, c in class_pairs("sc")]
+        return [p for p in pairs if all(kind == "c" or mirrored(v) for kind, v in zip(kinds, p))]
+
+    def split_columns(table, rows, cols):
+        full = np.zeros((rows, cols))
+        full[: table.shape[0], : table.shape[1]] = table
+        high, low = split_table(full)
+        return np.concatenate([high, high, low], axis=1)
 
     n_place = round_up(len(place), ROWS)
     n_pairs = round_up(len(pairs), ROWS)
     n_picked = round_up(len(picked), ROWS)
-
-    def stack(tables, rows, cols):
-        full = np.zeros((4, rows, cols))
-        for at, table in enumerate(tables):
-            full[at, : table.shape[0], : table.shape[1]] = table
-        high, low = split_table(full)
-        return np.concatenate([high, high, low], axis=2)
-
     scale = points**-1.5
-    small = class_waves(picked)
-    large = class_waves(pairs)
-    synth = stack([t.T * scale for t in small], n_place, n_picked)
-    project = stack(
-        [-t * place_weight * scale * (points / grid) ** 2 for t in small], n_picked, n_place
-    )
-    forward = stack([t * place_weight for t in large], n_pairs, n_place)
-    inverse = stack([t.T for t in large], n_place, n_pairs)
+    by_parity = dict(synth=[], project=[], forward=[], inverse=[])
+    for kinds in PARITIES:
+        few = class_waves(kinds, picked)
+        many = class_waves(kinds, class_pairs(kinds))
+        rows, depth = n_pairs, n_place
+        if small:
+            rows = round_up(many.shape[0], ROWS)
+            depth = round_up(1 + np.flatnonzero(np.abs(many).max(axis=0) > 1e-9)[-1], ROWS)
+        few_back = -few * place_weight * scale * (points / grid) ** 2
+        by_parity["synth"].append(split_columns(few.T * scale, n_place, n_picked))
+        by_parity["project"].append(split_columns(few_back, n_picked, n_place))
+        by_parity["forward"].append(split_columns((many * place_weight)[:, :depth], rows, depth))
+        by_parity["inverse"].append(split_columns(many.T, n_place, rows))
 
     index = np.arange(points)
     angle = 2.0 * np.pi * ((index[:, None] * index[None, :]) % points) / points
@@ -106,7 +120,7 @@
     scaled = total / screen_width
     safe = np.where(total > 0, scaled, 1.0)
     kernel = kernel_scale * np.where(total > 0, -np.expm1(-safe) / safe, 1.0)
-    double = np.where(2 * freqs % grid == 0, 1.0, 2.0)
+    double = np.where(mirrored(freqs), 2.0, 1.0)
     kernel = kernel * (double[:, 0] * double[:, 1])[:, None]
     kernel = kernel * (points / grid) ** 2 / float(points**3)
     weights = np.zeros((n_pairs, lanes))
@@ -116,61 +130,50 @@
     codes = np.full((n_picked, LANES), -7.0)
     for at, (b, c) in enumerate(picked):
         codes[at, 0], codes[at, 1] = b, c
-    return dict(
-        synth=synth,
-        project=project,
-        forward=forward,
-        inverse=inverse,
+    tables = dict(
         turn_left=turn_left,
         turn_right=turn_right,
         weights=np.concatenate(split_table(weights), axis=1),
         codes=codes.astype(ml_dtypes.bfloat16),
     )
+    for name, each in by_parity.items():
+        if small:
+            tables.update({name + str(at): table for at, table in enumerate(each)})
+        else:
+            tables[name] = np.stack(each)
+    return tables, small
 
 
 def pack_tables(tables):
-    shelves = (("forward",), ("project",), ("inverse", "synth"))
-    shelves += (("turn_left", "turn_right", "weights", "codes"),)
-    flat = {name: table.reshape(-1, table.shape[-1]) for name, table in tables.items()}
+    parities = [str(at) for at in range(len(PARITIES))]
+    shelves = [("forward" + at,) for at in parities] + [("project" + at,) for at in parities]
+    shelves += [("inverse" + at, "synth" + at) for at in parities]
+    shelves.append(("turn_left", "turn_right", "weights", "codes"))
     where, row, width = {}, 0, 0
     for shelf in shelves:
         column = 0
         for name in shelf:
             where[name] = (row, column)
-            column += round_up(flat[name].shape[1], LANES)
-        row += round_up(max(flat[name].shape[0] for name in shelf), ROWS)
+            column += round_up(tables[name].shape[1], LANES)
+        row += round_up(max(tables[name].shape[0] for name in shelf), ROWS)
         width = max(width, column)
     packed = np.zeros((row, width), ml_dtypes.bfloat16)
     for name, (first, column) in where.items():
-        rows, cols = flat[name].shape
-        packed[first : first + rows, column : column + cols] = flat[name]
+        rows, cols = tables[name].shape
+        packed[first : first + rows, column : column + cols] = tables[name]
     return packed, where
 
 
 def table_getter(shapes, refs, where):
     def get(name, at=None):
-        shape = shapes[name]
         if where is None:
-            ref = refs[TABLE_NAMES.index(name)]
+            ref = refs[list(shapes).index(name)]
             return ref[...] if at is None else ref[at]
-        first, column = where[name]
-        rows = shape[-2]
-        first = first if at is None else first + at * rows
-        return refs[0][first : first + rows, column : column + shape[-1]]
+        name = name if at is None else name + str(at)
+        (first, column), (rows, cols) = where[name], shapes[name]
+        return refs[0][first : first + rows, column : column + cols]
 
     return get
-
-
-TABLE_NAMES = (
-    "synth",
-    "project",
-    "forward",
-    "inverse",
-    "turn_left",
-    "turn_right",
-    "weights",
-    "codes",
-)
 
 
 def dot(left, right):
@@ -249,16 +252,16 @@
         orbs_ref[at] = quadrant
 
 
-def exchange_kernel(members, points, sizes, begins, ends, shapes, where, *refs):
+def exchange_kernel(members, points, owners, sizes, begins, ends, shapes, where, *refs):
     refs = list(refs)
     take = lambda count: [refs.pop(0) for _ in range(count)]
     prior_ref = None
     if begins:
-        indices_ref, flag_in_ref = take(2)
+        *indices_refs, flag_in_ref = take(owners + 1)
     else:
         pick_ref, own_ref, prior_ref = take(3)
     coef_refs = take(sum(sizes))
-    get = table_getter(shapes, take(len(TABLE_NAMES) if where is None else 1), where)
+    get = table_getter(shapes, take(len(shapes) if where is None else 1), where)
     if ends:
         (out_ref,) = take(1)
     elif begins:
@@ -270,7 +273,7 @@
     if begins and ends:
         pick_ref, own_ref, field_ref = take(3)
     if begins:
-        pick_ref[...] = pick_matrix(indices_ref[...], get("codes").astype(jnp.float32), points)
+        pick_ref[...] = pick_matrix(jnp.concatenate([ref[...] for ref in indices_refs], axis=1), get("codes").astype(jnp.float32), points)
     pick, turn_right = pick_ref[...], get("turn_right")
     lanes = turn_right.shape[0] // 2
     pad = lanes - members * points
@@ -300,13 +303,18 @@
             density.append(jnp.concatenate([own_ref[at]] * size, axis=1) * visit_ref[at])
         density = unfold(density)
         if small:
-            spectra = [product(get("forward", at), density[at]) for at in range(4)]
+            spectra = []
+            for at in range(4):
+                table = get("forward", at)
+                spectra.append(product(table, density[at][: table.shape[1] // 3]))
+            rows = [part.shape[0] for part in spectra]
             spectrum = turn(jnp.concatenate(spectra, axis=0), turn_right)
-            spectrum = turn(spectrum * jnp.concatenate([weights] * 4, axis=0), turn_right)
-            rows = weights.shape[0]
-            potential = [
-                product(get("inverse", at), spectrum[at * rows : (at + 1) * rows]) for at in range(4)
-            ]
+            spectrum = spectrum * jnp.concatenate([weights[:count] for count in rows], axis=0)
+            spectrum = turn(spectrum, turn_right)
+            potential = []
+            for at in range(4):
+                first = sum(rows[:at])
+                potential.append(product(get("inverse", at), spectrum[first : first + rows[at]]))
         else:
             for at, part in enumerate(density):
                 work_ref[at] = part
@@ -342,7 +350,7 @@
         out_ref[...] = result[: members * points]
 
 
-def load_kernel(*refs):
+def hold_kernel(*refs):
     semaphores = refs[-1]
     count = (len(refs) - 1) // 2
     copies = [
@@ -354,14 +362,14 @@
         copy.wait()
 
 
-def load(values):
+def hold(*values):
     return pl.pallas_call(
-        load_kernel,
+        hold_kernel,
         out_shape=[jax.ShapeDtypeStruct(value.shape, value.dtype) for value in values],
         in_specs=[pl.BlockSpec(memory_space=pl.ANY)] * len(values),
         out_specs=[pl.BlockSpec(memory_space=pltpu.VMEM)] * len(values),
         scratch_shapes=[pltpu.SemaphoreType.DMA((len(values),))],
-        cost_estimate=pl.CostEstimate(flops=0, bytes_accessed=2**20, transcendentals=0),
+        cost_estimate=pl.CostEstimate(flops=5 * 10**9, bytes_accessed=2**20, transcendentals=0),
         compiler_params=pltpu.CompilerParams(vmem_limit_bytes=16 * 2**20),
     )(*values)
 
@@ -383,23 +391,21 @@
     groups, members, points, per_owner = stick_coefs.shape
     owners = lax.axis_size("pw")
     batch = max(n for n in range(1, members + 1) if members % n == 0 and (n == 1 or n * points <= LANES))
-    tables = build_tables(points, per_owner * owners, batch)
+    tables, small = build_tables(points, per_owner * owners, batch)
     shapes = {name: table.shape for name, table in tables.items()}
-    small = tables["inverse"].shape[1] <= SMALL
-    where = None
+    where, held = None, list(tables.values())
     if small:
         packed, where = pack_tables(tables)
-        values = [jnp.asarray(packed)]
-    else:
-        values = [jnp.asarray(tables[name]) for name in TABLE_NAMES]
+        held = [packed]
+    values = [jnp.asarray(table) for table in held]
     own = stick_coefs.reshape(members * points, per_owner)
     others = rest_of_ring(own, "pw")
-    if batch == members:
-        (own,) = load([own])
     position = jnp.arange(per_owner, dtype=jnp.int32)[None]
     indices = jnp.where(position < stick_count[0], miller, -1).astype(jnp.float32)
     indices = jnp.concatenate([indices, jnp.zeros((6, per_owner), jnp.float32)], axis=0)
-    indices = jnp.concatenate([indices] + rest_of_ring(indices, "pw"), axis=1)
+    other_indices = rest_of_ring(indices, "pw")
+    own, indices = hold(own, indices)
+    indices = [indices] + other_indices
 
     ring = lax.axis_size("band")
     coefs = jnp.stack([own] + others)
@@ -407,7 +413,7 @@
     got = swap(jnp.stack([coefs, mate]), "band", lambda at: at + 1 if at & 1 else at - 1 + ring)
 
     lanes = tables["turn_right"].shape[0] // 2
-    n_place, n_picked = tables["synth"].shape[1], tables["project"].shape[1]
+    n_place, n_picked = shapes["synth0" if small else "synth"][-2], shapes["codes"][0]
     vmem = pl.BlockSpec(memory_space=pltpu.VMEM)
     grid_shape = jax.ShapeDtypeStruct((4, n_place, lanes), jnp.float32)
 
@@ -424,7 +430,7 @@
         if begins and ends:
             scratch += [pltpu.VMEM(each.shape, each.dtype) for each in (pick_shape, grid_shape, grid_shape)]
         return pl.pallas_call(
-            functools.partial(exchange_kernel, batch, points, sizes, begins, ends, shapes, where),
+            functools.partial(exchange_kernel, batch, points, owners, sizes, begins, ends, shapes, where),
             out_shape=out_shape,
             in_specs=[vmem] * (len(carried) + len(groups_in) + len(values)),
             out_specs=jax.tree.map(lambda _: vmem, out_shape),
@@ -437,7 +443,7 @@
     if small and batch == members:
         pick, orbs, field, flag = call(
             (2,),
-            (indices, flag),
+            (*indices, flag),
             (coefs, mate),
             (pick_shape, grid_shape, grid_shape, jax.ShapeDtypeStruct(flag.shape, flag.dtype)),
             begins=True,
@@ -449,7 +455,7 @@
         last = swap(got[0], "band", lambda at: at ^ 1)
 
         def exchange(pieces):
-            return call((2, 2, 1), (indices, flag), pieces, out_shape, begins=True, ends=True)
+            return call((2, 2, 1), (*indices, flag), pieces, out_shape, begins=True, ends=True)
 
         def cut(piece):
             return piece.reshape(owners, -1, batch * points, per_owner).swapaxes(0, 1)

time: 26.6 us -> 23.2 us (0.87)
  local copies, waits for them, and re-layouts: 3.88 us -> 0.83 us
  Pallas kernels: 11.5 us -> 10.8 us
  waiting for transfers between devices: 0.95 us -> 1.44 us
    unnamed x6 -> x4, local copies, waits for them, and re-layouts: 3.86 us -> 0.8 us
    ppermute x3, starting transfers between devices: 6.4 us -> 4.6 us  [swap(): lax.ppermute(value, axis, [(at, partner(at) % count) for at in range(coun...]
    ppermute x2, starting transfers between devices: 2.04 us -> 3.8 us  [rest_of_ring(): lax.ppermute(value, axis, [(at, (at + step) % count) for at in range(coun...]
    ppermute x3, waiting for transfers between devices: 0.45 us -> 1.44 us  [swap(): lax.ppermute(value, axis, [(at, partner(at) % count) for at in range(coun...]
    pallas_call x4, Pallas kernels: 11.5 us -> 10.8 us  [the longest x3 10.8 us: call(): pl.pallas_call(functools.partial(exchange_kernel, batch, points, owners,...]
    ppermute x2, waiting for transfers between devices: 0.5 us -> 0.01 us  [rest_of_ring(): lax.ppermute(value, axis, [(at, (at + step) % count) for at in range(coun...]
  transfers between devices with their start and end apart: 5 -> 5, of which waited for: 2 -> 1; matrix products, arithmetic and copies ran while one was open for 3% -> 3% of each run, Pallas kernels for 27% -> 29%
where the time goes in v2:
time: 23.2 us; the launch traced here: 23 us
  Pallas kernels  10.8 us (47%)
  starting transfers between devices  8.4 us (36%)
  waiting for transfers between devices  1.44 us (6%)
  local copies, waits for them, and re-layouts  0.83 us (4%)
  other arithmetic  0.75 us (3%)
  between operations  0.73 us (3%)
    pallas_call x3, Pallas kernels, call(): pl.pallas_call(functools.partial(exchange_kernel, batch, points, owners,...  10.8 us
    ppermute x3, starting transfers between devices, swap(): lax.ppermute(value, axis, [(at, partner(at) % count) for at in range(coun...  4.6 us
    ppermute x2, starting transfers between devices, rest_of_ring(): lax.ppermute(value, axis, [(at, (at + step) % count) for at in range(coun...  3.8 us
    ppermute x3, waiting for transfers between devices, swap(): lax.ppermute(value, axis, [(at, partner(at) % count) for at in range(coun...  1.44 us
    unnamed x4, local copies, waits for them, and re-layouts  0.8 us
    convert_element_type x1, other arithmetic, shards(): jnp.where(position < stick_count[0], miller, -1).astype(jnp.float32)  0.69 us
  transfers between devices with their start and end apart: 5, of which 1 were waited for; matrix products, arithmetic and copies ran while one was open for 3% of the time, Pallas kernels for 29%

profile of v2, /device:TPU:1, one launch (start us, length us, event | category | flops | bytes accessed | tf_op | source)
XLA Modules:
  0.0 23.0 jit_solution(11126987251593938691)
XLA Ops:
  0.0 2.0 %collective-permute-start.1 = (f32[96,128]{1,0:T(8,128)}, f32[96,128]{1,0:T(8,128)S(1)}, u32[]{:S(2)}, u32[]{:S(2)}) collective-permute-start(f32[96,128]{1,0:T(8,128)} %bitcast.17), channel_id=1, source_target_pairs={{0,16},{16,0},{1,17},{17,1},{2,18},{18,2},{3,19},{19,3},{4,20},{20... | collective-permute-start | bytes 147464 | tf_op jit(solution)/shard_map/ppermute | solution.py:385
  2.7 0.7 %select_convert_fusion = f32[2,128]{1,0:T(2,128)S(1)} fusion(s32[2,128]{1,0:T(2,128)} %param.5, pred[128]{0:T(512)(128)(4,1)S(1)} %iota_compare_fusion), kind=kLoop, calls=%fused_computation.6 | loop fusion | flops 512 | bytes 2176 | tf_op jit(solution)/shard_map/convert_element_type | solution.py:404
  3.4 0.0 copy-start
  3.4 0.8 %copy-done = f32[1,2,48,128]{3,2,1,0:T(8,128)S(1)} copy-done((f32[1,2,48,128]{3,2,1,0:T(8,128)S(1)}, f32[1,2,48,128]{3,2,1,0:T(8,128)}, u32[]{:S(2)}) %copy-start) | copy-done | bytes 49176
  4.2 0.0 copy-start.1
  4.2 0.1 shard_map.46
  4.3 0.0 collective-permute-done.1
  4.3 1.1 %collective-permute-start.2 = (f32[2,96,128]{2,1,0:T(8,128)S(1)}, f32[2,96,128]{2,1,0:T(8,128)S(1)}, u32[]{:S(2)}, u32[]{:S(2)}) collective-permute-start(f32[2,96,128]{2,1,0:T(8,128)S(1)} %get-tuple-element.20.refs_3_), channel_id=1, source_target_pairs={{0,1},{1,0},{2,3},{3,2},{4,5},{5,4},{6,7},{7,6},{8,9},{9,8},{10,11... | collective-permute-start | bytes 294920 | tf_op jit(solution)/shard_map/ppermute | solution.py:379
  5.4 1.8 %collective-permute-start = (f32[8,128]{1,0:T(8,128)S(1)}, f32[8,128]{1,0:T(8,128)S(1)}, u32[]{:S(2)}, u32[]{:S(2)}) collective-permute-start(f32[8,128]{1,0:T(8,128)S(1)} %concatenate.3.refs_1_), channel_id=1, source_target_pairs={{0,16},{16,0},{1,17},{17,1},{2,18},{18,2},{3,19},{19,3},{4,20},{20... | collective-permute-start | bytes 12296 | tf_op jit(solution)/shard_map/ppermute | solution.py:385
  7.1 0.0 collective-permute-done.2.refs_4_
  7.1 1.5 %collective-permute-start.3 = (f32[2,2,96,128]{3,2,1,0:T(8,128)S(1)}, f32[2,2,96,128]{3,2,1,0:T(8,128)S(1)}, u32[]{:S(2)}, u32[]{:S(2)}) collective-permute-start(f32[2,2,96,128]{3,2,1,0:T(8,128)S(1)} %pad_maximum_fusion), channel_id=1, source_target_pairs={{0,15},{1,2},{2,1},{3,4},{4,3},{5,6},{6,5},{7,8},{8,7},{9,10},{10,... | collective-permute-start | bytes 589832 | tf_op jit(solution)/shard_map/ppermute | solution.py:379
  8.7 0.0 collective-permute-done.refs_1_
  8.7 0.0 copy-done.1
  8.7 3.3 %shard_map.47 = (bf16[320,256]{1,0:T(8,128)(2,1)S(1)}, f32[4,368,128]{2,1,0:T(8,128)S(1)}, f32[4,368,128]{2,1,0:T(8,128)S(1)}, f32[96,128]{1,0:T(8,128)S(1)}) custom-call(f32[8,128]{1,0:T(8,128)S(1)} %get-tuple-element.11.refs_0_, f32[8,128]{1,0:T(8,128)S(1)} %collective-permute-done.refs_1_, f32[96,128]{1,0:T(8,128)S(1)} %broadcast_in_dim.27.refs_2_, ...), custom_call_target="tpu_custom_call" | custom-call | flops 5000000000 | bytes 4194304 | tf_op jit(solution)/shard_map/pallas_call | solution.py:432
  12.0 1.4 %collective-permute-done.3 = f32[2,2,96,128]{3,2,1,0:T(8,128)S(1)} collective-permute-done((f32[2,2,96,128]{3,2,1,0:T(8,128)S(1)}, f32[2,2,96,128]{3,2,1,0:T(8,128)S(1)}, u32[]{:S(2)}, u32[]{:S(2)}) %collective-permute-start.3) | collective-permute-done | bytes 196640 | tf_op jit(solution)/shard_map/ppermute | solution.py:379
  13.4 2.0 %collective-permute-start.4 = (f32[2,96,128]{2,1,0:T(8,128)S(1)}, f32[2,96,128]{2,1,0:T(8,128)S(1)}, u32[]{:S(2)}, u32[]{:S(2)}) collective-permute-start(f32[2,96,128]{2,1,0:T(8,128)S(1)} %broadcast_select_fusion), channel_id=1, source_target_pairs={{0,1},{1,0},{2,3},{3,2},{4,5},{5,4},{6,7},{7,6},{8,9},{9,8},{10,11... | collective-permute-start | bytes 294920 | tf_op jit(solution)/shard_map/ppermute | solution.py:379
  15.4 3.3 %shard_map.48.refs_2_ = f32[4,368,128]{2,1,0:T(8,128)S(1)} custom-call(bf16[320,256]{1,0:T(8,128)(2,1)S(1)} %get-tuple-element.13.refs_0_, f32[4,368,128]{2,1,0:T(8,128)S(1)} %get-tuple-element.14.refs_1_, f32[4,368,128]{2,1,0:T(8,128)S(1)} %get-tuple-element.15.refs_2_, f32[2,96,128]{2,1,0:T(8,128)S(1)} %get-tuple-element.18.refs_3_, ...), custom_call_target="tpu_custom_call" | custom-call | flops 5000000000 | bytes 4194304 | tf_op jit(solution)/shard_map/pallas_call | solution.py:432
  18.7 0.0 collective-permute-done.4.refs_3_
  18.8 4.2 %shard_map.49 = f32[96,128]{1,0:T(8,128)} custom-call(bf16[320,256]{1,0:T(8,128)(2,1)S(1)} %get-tuple-element.13.refs_0_, f32[4,368,128]{2,1,0:T(8,128)S(1)} %get-tuple-element.14.refs_1_, f32[4,368,128]{2,1,0:T(8,128)S(1)} %shard_map.48.refs_2_, f32[2,96,128]{2,1,0:T(8,128)S(1)} %collective-permute-done.4.refs_3_, bf16[3088,1152]{1,0:T(8,128)(2,1)S(1)} %copy-done.1), custom_call_target="tpu_custom_call" | custom-call | flops 5000000000 | bytes 4194304 | tf_op jit(solution)/shard_map/pallas_call | solution.py:432
  (8 shorter events, 0.1 us)
Async XLA Ops:
  0.0 4.3 %collective-permute-start.1 = (f32[96,128]{1,0:T(8,128)}, f32[96,128]{1,0:T(8,128)S(1)}, u32[]{:S(2)}, u32[]{:S(2)}) collective-permute-start(f32[96,128]{1,0:T(8,128)} %bitcast.17), channel_id=1, source_target_pairs={{0,16},{16,0},{1,17},{17,1},{2,18},{18,2},{3,19},{19,3},{4,20},{20... | collective-permute-start | bytes 147464 | tf_op jit(solution)/shard_map/ppermute | solution.py:385
  3.4 0.8 %copy-start = (f32[1,2,48,128]{3,2,1,0:T(8,128)S(1)}, f32[1,2,48,128]{3,2,1,0:T(8,128)}, u32[]{:S(2)}) copy-start(f32[1,2,48,128]{3,2,1,0:T(8,128)} %param.4) | copy-start | bytes 147460
  4.2 4.5 %copy-start.1 = (bf16[3088,1152]{1,0:T(8,128)(2,1)S(1)}, bf16[3088,1152]{1,0:T(8,128)(2,1)}, u32[]{:S(2)}) copy-start(bf16[3088,1152]{1,0:T(8,128)(2,1)} %constant.2.clone.refs_5_.refs_4_) | copy-start | bytes 21344260
  4.3 2.8 %collective-permute-start.2 = (f32[2,96,128]{2,1,0:T(8,128)S(1)}, f32[2,96,128]{2,1,0:T(8,128)S(1)}, u32[]{:S(2)}, u32[]{:S(2)}) collective-permute-start(f32[2,96,128]{2,1,0:T(8,128)S(1)} %get-tuple-element.20.refs_3_), channel_id=1, source_target_pairs={{0,1},{1,0},{2,3},{3,2},{4,5},{5,4},{6,7},{7,6},{8,9},{9,8},{10,11... | collective-permute-start | bytes 294920 | tf_op jit(solution)/shard_map/ppermute | solution.py:379
  5.4 3.3 %collective-permute-start = (f32[8,128]{1,0:T(8,128)S(1)}, f32[8,128]{1,0:T(8,128)S(1)}, u32[]{:S(2)}, u32[]{:S(2)}) collective-permute-start(f32[8,128]{1,0:T(8,128)S(1)} %concatenate.3.refs_1_), channel_id=1, source_target_pairs={{0,16},{16,0},{1,17},{17,1},{2,18},{18,2},{3,19},{19,3},{4,20},{20... | collective-permute-start | bytes 12296 | tf_op jit(solution)/shard_map/ppermute | solution.py:385
  7.1 6.3 %collective-permute-start.3 = (f32[2,2,96,128]{3,2,1,0:T(8,128)S(1)}, f32[2,2,96,128]{3,2,1,0:T(8,128)S(1)}, u32[]{:S(2)}, u32[]{:S(2)}) collective-permute-start(f32[2,2,96,128]{3,2,1,0:T(8,128)S(1)} %pad_maximum_fusion), channel_id=1, source_target_pairs={{0,15},{1,2},{2,1},{3,4},{4,3},{5,6},{6,5},{7,8},{8,7},{9,10},{10,... | collective-permute-start | bytes 589832 | tf_op jit(solution)/shard_map/ppermute | solution.py:379
  13.4 5.3 %collective-permute-start.4 = (f32[2,96,128]{2,1,0:T(8,128)S(1)}, f32[2,96,128]{2,1,0:T(8,128)S(1)}, u32[]{:S(2)}, u32[]{:S(2)}) collective-permute-start(f32[2,96,128]{2,1,0:T(8,128)S(1)} %broadcast_select_fusion), channel_id=1, source_target_pairs={{0,1},{1,0},{2,3},{3,2},{4,5},{5,4},{6,7},{7,6},{8,9},{9,8},{10,11... | collective-permute-start | bytes 294920 | tf_op jit(solution)/shard_map/ppermute | solution.py:379

commit v3 on v2

--- a/solution.py
+++ b/solution.py
@@ -192,7 +192,12 @@
 
 
 def product(table, value):
-    return dot(table, stacked(value))
+    depth, lanes = value.shape
+    if lanes > LANES or depth <= LANES:
+        return dot(table, stacked(value))
+    high, low = split(value)
+    out = dot(table[:, :depth], jnp.concatenate([high, low], axis=1))
+    return out[:, :lanes] + out[:, lanes:] + dot(table[:, 2 * depth :], high)
 
 
 def pick_matrix(indices, codes, points):
@@ -252,12 +257,31 @@
         orbs_ref[at] = quadrant
 
 
-def exchange_kernel(members, points, owners, sizes, begins, ends, shapes, where, *refs):
+def read_coefs(ref, lanes):
+    block = jnp.concatenate([ref[at] for at in range(ref.shape[0])], axis=1)
+    pad = lanes - block.shape[0]
+    if pad:
+        block = jnp.concatenate([block, jnp.zeros((pad, block.shape[1]), block.dtype)], axis=0)
+    return block
+
+
+def orbitals_kernel(count, shapes, where, pick_ref, *refs):
+    get = table_getter(shapes, refs[count:-count - 2], where)
+    out_refs, (all_ref, coefs_ref) = refs[-count - 2 : -2], refs[-2:]
+    lanes = get("turn_right").shape[0] // 2
+    blocks = [read_coefs(ref, lanes) for ref in refs[:count]]
+    synthesize(True, blocks, pick_ref[...], get, coefs_ref, all_ref)
+    for at in range(4):
+        for block, out_ref in enumerate(out_refs):
+            out_ref[at] = all_ref[at, :, block * lanes : (block + 1) * lanes]
+
+
+def exchange_kernel(members, points, owners, sizes, begins, ends, ready, shapes, where, *refs):
     refs = list(refs)
     take = lambda count: [refs.pop(0) for _ in range(count)]
     prior_ref = None
     if begins:
-        *indices_refs, flag_in_ref = take(owners + 1)
+        indices_refs = take(owners)
     else:
         pick_ref, own_ref, prior_ref = take(3)
     coef_refs = take(sum(sizes))
@@ -265,8 +289,7 @@
     if ends:
         (out_ref,) = take(1)
     elif begins:
-        pick_ref, own_ref, field_ref, flag_ref = take(4)
-        flag_ref[...] = flag_in_ref[...]
+        pick_ref, own_ref, field_ref = take(3)
     else:
         (field_ref,) = take(1)
     visit_all_ref, work_all_ref, coefs_all_ref = take(3)
@@ -276,31 +299,28 @@
         pick_ref[...] = pick_matrix(jnp.concatenate([ref[...] for ref in indices_refs], axis=1), get("codes").astype(jnp.float32), points)
     pick, turn_right = pick_ref[...], get("turn_right")
     lanes = turn_right.shape[0] // 2
-    pad = lanes - members * points
     small = where is not None
-
-    def coefs_of(ref):
-        block = jnp.concatenate([ref[at] for at in range(ref.shape[0])], axis=1)
-        if pad:
-            block = jnp.concatenate([block, jnp.zeros((pad, block.shape[1]), block.dtype)], axis=0)
-        return block
-
     weight = get("weights").astype(jnp.float32)
     weight = weight[:, :lanes] + weight[:, lanes:]
     start = 0
     for step, size in enumerate(sizes):
         refs = [ref.at[:, :, : size * lanes] for ref in (visit_all_ref, work_all_ref, coefs_all_ref)]
         visit_ref, work_ref, coefs_ref = refs
-        blocks = [coefs_of(ref) for ref in coef_refs[start : start + size]]
+        group_refs = coef_refs[start : start + size]
         start += size
-        synthesize(small, blocks, pick, get, coefs_ref, visit_ref)
+        if ready:
+            visit = [jnp.concatenate([ref[at] for ref in group_refs], axis=1) for at in range(4)]
+        else:
+            blocks = [read_coefs(ref, lanes) for ref in group_refs]
+            synthesize(small, blocks, pick, get, coefs_ref, visit_ref)
+            visit = [visit_ref[at] for at in range(4)]
         if begins and step == 0:
             for at in range(4):
                 own_ref[at] = visit_ref[at, :, :lanes]
         weights = jnp.concatenate([weight] * size, axis=1)
         density = []
         for at in range(4):
-            density.append(jnp.concatenate([own_ref[at]] * size, axis=1) * visit_ref[at])
+            density.append(jnp.concatenate([own_ref[at]] * size, axis=1) * visit[at])
         density = unfold(density)
         if small:
             spectra = []
@@ -328,7 +348,7 @@
             potential = [work_ref[at] for at in range(4)]
         field = []
         for at, quadrant in enumerate(unfold(potential)):
-            term = quadrant * visit_ref[at]
+            term = quadrant * visit[at]
             total = term[:, :lanes]
             for block in range(1, size):
                 total = total + term[:, block * lanes : (block + 1) * lanes]
@@ -420,7 +440,7 @@
     pick_shape = jax.ShapeDtypeStruct((4 * n_picked, per_owner * owners), jnp.bfloat16)
     out_shape = jax.ShapeDtypeStruct((batch * points, per_owner), jnp.float32)
 
-    def call(sizes, carried, groups_in, out_shape, begins=False, ends=False):
+    def call(sizes, carried, groups_in, out_shape, begins=False, ends=False, ready=False):
         wide = max(sizes) * lanes
         scratch = [
             pltpu.VMEM((4, n_place, wide), jnp.float32),
@@ -430,7 +450,9 @@
         if begins and ends:
             scratch += [pltpu.VMEM(each.shape, each.dtype) for each in (pick_shape, grid_shape, grid_shape)]
         return pl.pallas_call(
-            functools.partial(exchange_kernel, batch, points, owners, sizes, begins, ends, shapes, where),
+            functools.partial(
+                exchange_kernel, batch, points, owners, sizes, begins, ends, ready, shapes, where
+            ),
             out_shape=out_shape,
             in_specs=[vmem] * (len(carried) + len(groups_in) + len(values)),
             out_specs=jax.tree.map(lambda _: vmem, out_shape),
@@ -439,23 +461,34 @@
             compiler_params=pltpu.CompilerParams(vmem_limit_bytes=(24 if small else 50) * 2**20),
         )(*carried, *groups_in, *values)
 
-    flag = jnp.ones((batch * points, per_owner), jnp.float32)
+    def orbitals_of(pick, groups_in):
+        count = len(groups_in)
+        return pl.pallas_call(
+            functools.partial(orbitals_kernel, count, shapes, where),
+            out_shape=[grid_shape] * count,
+            in_specs=[vmem] * (1 + count + len(values)),
+            out_specs=[vmem] * count,
+            scratch_shapes=[
+                pltpu.VMEM((4, n_place, count * lanes), jnp.float32),
+                pltpu.VMEM((4, n_picked, count * lanes), jnp.float32),
+            ],
+            cost_estimate=pl.CostEstimate(flops=10**9, bytes_accessed=2**20, transcendentals=0),
+            compiler_params=pltpu.CompilerParams(vmem_limit_bytes=24 * 2**20),
+        )(pick, *groups_in, *values)
+
     if small and batch == members:
-        pick, orbs, field, flag = call(
-            (2,),
-            (*indices, flag),
-            (coefs, mate),
-            (pick_shape, grid_shape, grid_shape, jax.ShapeDtypeStruct(flag.shape, flag.dtype)),
-            begins=True,
+        pick, orbs, field = call(
+            (2,), indices, (coefs, mate), (pick_shape, grid_shape, grid_shape), begins=True
         )
-        last = swap(jnp.where(flag > 0.0, got[0], 0.0), "band", lambda at: at ^ 1)
-        field = call((2,), (pick, orbs, field), (got[0], got[1]), grid_shape)
-        result = call((1,), (pick, orbs, field), (last,), out_shape, ends=True)
+        near, far = orbitals_of(pick, (got[0], got[1]))
+        last = swap(near, "band", lambda at: at ^ 1)
+        field = call((2,), (pick, orbs, field), (near, far), grid_shape, ready=True)
+        result = call((1,), (pick, orbs, field), (last,), out_shape, ends=True, ready=True)
     else:
         last = swap(got[0], "band", lambda at: at ^ 1)
 
         def exchange(pieces):
-            return call((2, 2, 1), (*indices, flag), pieces, out_shape, begins=True, ends=True)
+            return call((2, 2, 1), indices, pieces, out_shape, begins=True, ends=True)
 
         def cut(piece):
             return piece.reshape(owners, -1, batch * points, per_owner).swapaxes(0, 1)

time: 23.2 us -> 22.1 us (0.953)
  Pallas kernels: 10.8 us -> 9.72 us
    pallas_call x3, Pallas kernels: 10.8 us -> 8.71 us  [call(): pl.pallas_call(functools.partial(exchange_kernel, batch, points, owners,...]
    pallas_call x0 -> x1, Pallas kernels: none -> 0.94 us  [orbitals_of(): pl.pallas_call(functools.partial(orbitals_kernel, count, shapes, where),...]
  transfers between devices with their start and end apart: 5 -> 5, of which waited for: 1 -> 1; matrix products, arithmetic and copies ran while one was open for 3% -> 3% of each run, Pallas kernels for 29% -> 26%
where the time goes in v3:
time: 22.1 us; the launch traced here: 21.9 us
  Pallas kernels  9.72 us (44%)
  starting transfers between devices  8.39 us (38%)
  waiting for transfers between devices  1.48 us (7%)
  local copies, waits for them, and re-layouts  0.82 us (4%)
  between operations  0.73 us (3%)
  other arithmetic  0.72 us (3%)
    pallas_call x3, Pallas kernels, call(): pl.pallas_call(functools.partial(exchange_kernel, batch, points, owners,...  8.71 us
    ppermute x3, starting transfers between devices, swap(): lax.ppermute(value, axis, [(at, partner(at) % count) for at in range(coun...  4.6 us
    ppermute x2, starting transfers between devices, rest_of_ring(): lax.ppermute(value, axis, [(at, (at + step) % count) for at in range(coun...  3.8 us
    ppermute x3, waiting for transfers between devices, swap(): lax.ppermute(value, axis, [(at, partner(at) % count) for at in range(coun...  1.48 us
    pallas_call x1, Pallas kernels, orbitals_of(): pl.pallas_call(functools.partial(orbitals_kernel, count, shapes, where),...  0.94 us
    unnamed x4, local copies, waits for them, and re-layouts  0.8 us
    convert_element_type x1, other arithmetic, shards(): jnp.where(position < stick_count[0], miller, -1).astype(jnp.float32)  0.69 us
  transfers between devices with their start and end apart: 5, of which 1 were waited for; matrix products, arithmetic and copies ran while one was open for 3% of the time, Pallas kernels for 26%

profile of v3, /device:TPU:1, one launch (start us, length us, event | category | flops | bytes accessed | tf_op | source)
XLA Modules:
  0.0 21.9 jit_solution(12846927450559351672)
XLA Ops:
  0.0 2.0 %collective-permute-start.1 = (f32[96,128]{1,0:T(8,128)}, f32[96,128]{1,0:T(8,128)S(1)}, u32[]{:S(2)}, u32[]{:S(2)}) collective-permute-start(f32[96,128]{1,0:T(8,128)} %bitcast.15), channel_id=1, source_target_pairs={{0,16},{16,0},{1,17},{17,1},{2,18},{18,2},{3,19},{19,3},{4,20},{20... | collective-permute-start | bytes 147464 | tf_op jit(solution)/shard_map/ppermute | solution.py:405
  2.7 0.7 %select_convert_fusion = f32[2,128]{1,0:T(2,128)S(1)} fusion(s32[2,128]{1,0:T(2,128)} %param.5, pred[128]{0:T(512)(128)(4,1)S(1)} %iota_compare_fusion), kind=kLoop, calls=%fused_computation.4 | loop fusion | flops 512 | bytes 2176 | tf_op jit(solution)/shard_map/convert_element_type | solution.py:424
  3.4 0.0 copy-start.1
  3.4 0.8 %copy-done.1 = f32[1,2,48,128]{3,2,1,0:T(8,128)S(1)} copy-done((f32[1,2,48,128]{3,2,1,0:T(8,128)S(1)}, f32[1,2,48,128]{3,2,1,0:T(8,128)}, u32[]{:S(2)}) %copy-start.1) | copy-done | bytes 49176
  4.2 0.0 copy-start
  4.2 0.1 shard_map.46
  4.3 0.0 collective-permute-done.1
  4.3 1.1 %collective-permute-start.2 = (f32[2,96,128]{2,1,0:T(8,128)S(1)}, f32[2,96,128]{2,1,0:T(8,128)S(1)}, u32[]{:S(2)}, u32[]{:S(2)}) collective-permute-start(f32[2,96,128]{2,1,0:T(8,128)S(1)} %get-tuple-element.22.refs_2_), channel_id=1, source_target_pairs={{0,1},{1,0},{2,3},{3,2},{4,5},{5,4},{6,7},{7,6},{8,9},{9,8},{10,11... | collective-permute-start | bytes 294920 | tf_op jit(solution)/shard_map/ppermute | solution.py:399
  5.4 1.8 %collective-permute-start = (f32[8,128]{1,0:T(8,128)S(1)}, f32[8,128]{1,0:T(8,128)S(1)}, u32[]{:S(2)}, u32[]{:S(2)}) collective-permute-start(f32[8,128]{1,0:T(8,128)S(1)} %concatenate.3.refs_1_), channel_id=1, source_target_pairs={{0,16},{16,0},{1,17},{17,1},{2,18},{18,2},{3,19},{19,3},{4,20},{20... | collective-permute-start | bytes 12296 | tf_op jit(solution)/shard_map/ppermute | solution.py:405
  7.1 0.0 collective-permute-done.2.refs_3_
  7.1 1.5 %collective-permute-start.3 = (f32[2,2,96,128]{3,2,1,0:T(8,128)S(1)}, f32[2,2,96,128]{3,2,1,0:T(8,128)S(1)}, u32[]{:S(2)}, u32[]{:S(2)}) collective-permute-start(f32[2,2,96,128]{3,2,1,0:T(8,128)S(1)} %pad_maximum_fusion), channel_id=1, source_target_pairs={{0,15},{1,2},{2,1},{3,4},{4,3},{5,6},{6,5},{7,8},{8,7},{9,10},{10,... | collective-permute-start | bytes 589832 | tf_op jit(solution)/shard_map/ppermute | solution.py:399
  8.7 0.0 collective-permute-done.refs_1_
  8.7 0.0 copy-done
  8.7 3.2 %shard_map.47 = (bf16[320,256]{1,0:T(8,128)(2,1)S(1)}, f32[4,368,128]{2,1,0:T(8,128)S(1)}, f32[4,368,128]{2,1,0:T(8,128)S(1)}) custom-call(f32[8,128]{1,0:T(8,128)S(1)} %get-tuple-element.12.refs_0_, f32[8,128]{1,0:T(8,128)S(1)} %collective-permute-done.refs_1_, f32[2,96,128]{2,1,0:T(8,128)S(1)} %get-tuple-element.22.refs_2_, ...), custom_call_target="tpu_custom_call" | custom-call | flops 5000000000 | bytes 4194304 | tf_op jit(solution)/shard_map/pallas_call | solution.py:452
  11.9 1.5 %collective-permute-done.3 = f32[2,2,96,128]{3,2,1,0:T(8,128)S(1)} collective-permute-done((f32[2,2,96,128]{3,2,1,0:T(8,128)S(1)}, f32[2,2,96,128]{3,2,1,0:T(8,128)S(1)}, u32[]{:S(2)}, u32[]{:S(2)}) %collective-permute-start.3) | collective-permute-done | bytes 196640 | tf_op jit(solution)/shard_map/ppermute | solution.py:399
  13.4 0.9 %shard_map.48 = (f32[4,368,128]{2,1,0:T(8,128)S(1)}, f32[4,368,128]{2,1,0:T(8,128)S(1)}) custom-call(bf16[320,256]{1,0:T(8,128)(2,1)S(1)} %get-tuple-element.14.pick_ref.refs_0_, f32[2,96,128]{2,1,0:T(8,128)S(1)} %get-tuple-element.20.refs_0_, f32[2,96,128]{2,1,0:T(8,128)S(1)} %get-tuple-element.19.refs_1_, bf16[3088,1152]{1,0:T(8,128)(2,1)S(1)} %copy-done), custom_call_target="tpu_custom_call" | custom-call | flops 1000000000 | bytes 1048576 | tf_op jit(solution)/shard_map/pallas_call | solution.py:466
  14.4 2.0 %collective-permute-start.4 = (f32[4,368,128]{2,1,0:T(8,128)S(1)}, f32[4,368,128]{2,1,0:T(8,128)S(1)}, u32[]{:S(2)}, u32[]{:S(2)}) collective-permute-start(f32[4,368,128]{2,1,0:T(8,128)S(1)} %get-tuple-element.17.refs_3_), channel_id=1, source_target_pairs={{0,1},{1,0},{2,3},{3,2},{4,5},{5,4},{6,7},{7,6},{8,9},{9,8},{10,11... | collective-permute-start | bytes 2261000 | tf_op jit(solution)/shard_map/ppermute | solution.py:399
  16.4 2.4 %shard_map.49.refs_2_ = f32[4,368,128]{2,1,0:T(8,128)S(1)} custom-call(bf16[320,256]{1,0:T(8,128)(2,1)S(1)} %get-tuple-element.14.pick_ref.refs_0_, f32[4,368,128]{2,1,0:T(8,128)S(1)} %get-tuple-element.15.refs_1_, f32[4,368,128]{2,1,0:T(8,128)S(1)} %get-tuple-element.16.refs_2_, f32[4,368,128]{2,1,0:T(8,128)S(1)} %get-tuple-element.17.refs_3_, ...), custom_call_target="tpu_custom_call" | custom-call | flops 5000000000 | bytes 4194304 | tf_op jit(solution)/shard_map/pallas_call | solution.py:452
  18.8 0.0 collective-permute-done.4.refs_3_
  18.8 3.1 %shard_map.50 = f32[96,128]{1,0:T(8,128)} custom-call(bf16[320,256]{1,0:T(8,128)(2,1)S(1)} %get-tuple-element.14.pick_ref.refs_0_, f32[4,368,128]{2,1,0:T(8,128)S(1)} %get-tuple-element.15.refs_1_, f32[4,368,128]{2,1,0:T(8,128)S(1)} %shard_map.49.refs_2_, f32[4,368,128]{2,1,0:T(8,128)S(1)} %collective-permute-done.4.refs_3_, bf16[3088,1152]{1,0:T(8,128)(2,1)S(1)} %copy-done), custom_call_target="tpu_custom_call" | custom-call | flops 5000000000 | bytes 4194304 | tf_op jit(solution)/shard_map/pallas_call | solution.py:452
  (5 shorter events, 0.1 us)
Async XLA Ops:
  0.0 4.3 %collective-permute-start.1 = (f32[96,128]{1,0:T(8,128)}, f32[96,128]{1,0:T(8,128)S(1)}, u32[]{:S(2)}, u32[]{:S(2)}) collective-permute-start(f32[96,128]{1,0:T(8,128)} %bitcast.15), channel_id=1, source_target_pairs={{0,16},{16,0},{1,17},{17,1},{2,18},{18,2},{3,19},{19,3},{4,20},{20... | collective-permute-start | bytes 147464 | tf_op jit(solution)/shard_map/ppermute | solution.py:405
  3.4 0.8 %copy-start.1 = (f32[1,2,48,128]{3,2,1,0:T(8,128)S(1)}, f32[1,2,48,128]{3,2,1,0:T(8,128)}, u32[]{:S(2)}) copy-start(f32[1,2,48,128]{3,2,1,0:T(8,128)} %param.4) | copy-start | bytes 147460
  4.2 4.5 %copy-start = (bf16[3088,1152]{1,0:T(8,128)(2,1)S(1)}, bf16[3088,1152]{1,0:T(8,128)(2,1)}, u32[]{:S(2)}) copy-start(bf16[3088,1152]{1,0:T(8,128)(2,1)} %constant.6.clone.refs_4_.refs_2_.refs_5_) | copy-start | bytes 21344260
  4.3 2.8 %collective-permute-start.2 = (f32[2,96,128]{2,1,0:T(8,128)S(1)}, f32[2,96,128]{2,1,0:T(8,128)S(1)}, u32[]{:S(2)}, u32[]{:S(2)}) collective-permute-start(f32[2,96,128]{2,1,0:T(8,128)S(1)} %get-tuple-element.22.refs_2_), channel_id=1, source_target_pairs={{0,1},{1,0},{2,3},{3,2},{4,5},{5,4},{6,7},{7,6},{8,9},{9,8},{10,11... | collective-permute-start | bytes 294920 | tf_op jit(solution)/shard_map/ppermute | solution.py:399
  5.4 3.3 %collective-permute-start = (f32[8,128]{1,0:T(8,128)S(1)}, f32[8,128]{1,0:T(8,128)S(1)}, u32[]{:S(2)}, u32[]{:S(2)}) collective-permute-start(f32[8,128]{1,0:T(8,128)S(1)} %concatenate.3.refs_1_), channel_id=1, source_target_pairs={{0,16},{16,0},{1,17},{17,1},{2,18},{18,2},{3,19},{19,3},{4,20},{20... | collective-permute-start | bytes 12296 | tf_op jit(solution)/shard_map/ppermute | solution.py:405
  7.1 6.3 %collective-permute-start.3 = (f32[2,2,96,128]{3,2,1,0:T(8,128)S(1)}, f32[2,2,96,128]{3,2,1,0:T(8,128)S(1)}, u32[]{:S(2)}, u32[]{:S(2)}) collective-permute-start(f32[2,2,96,128]{3,2,1,0:T(8,128)S(1)} %pad_maximum_fusion), channel_id=1, source_target_pairs={{0,15},{1,2},{2,1},{3,4},{4,3},{5,6},{6,5},{7,8},{8,7},{9,10},{10,... | collective-permute-start | bytes 589832 | tf_op jit(solution)/shard_map/ppermute | solution.py:399
  14.4 4.4 %collective-permute-start.4 = (f32[4,368,128]{2,1,0:T(8,128)S(1)}, f32[4,368,128]{2,1,0:T(8,128)S(1)}, u32[]{:S(2)}, u32[]{:S(2)}) collective-permute-start(f32[4,368,128]{2,1,0:T(8,128)S(1)} %get-tuple-element.17.refs_3_), channel_id=1, source_target_pairs={{0,1},{1,0},{2,3},{3,2},{4,5},{5,4},{6,7},{7,6},{8,9},{9,8},{10,11... | collective-permute-start | bytes 2261000 | tf_op jit(solution)/shard_map/ppermute | solution.py:399

commit v4 on v3

--- a/solution.py
+++ b/solution.py
@@ -323,18 +323,15 @@
             density.append(jnp.concatenate([own_ref[at]] * size, axis=1) * visit[at])
         density = unfold(density)
         if small:
-            spectra = []
-            for at in range(4):
-                table = get("forward", at)
-                spectra.append(product(table, density[at][: table.shape[1] // 3]))
-            rows = [part.shape[0] for part in spectra]
-            spectrum = turn(jnp.concatenate(spectra, axis=0), turn_right)
-            spectrum = spectrum * jnp.concatenate([weights[:count] for count in rows], axis=0)
-            spectrum = turn(spectrum, turn_right)
-            potential = []
-            for at in range(4):
-                first = sum(rows[:at])
-                potential.append(product(get("inverse", at), spectrum[first : first + rows[at]]))
+            stages = (
+                lambda at, part: product(get("forward", at), part[: get("forward", at).shape[1] // 3]),
+                lambda at, part: turn(part, turn_right) * weights[: part.shape[0]],
+                lambda at, part: turn(part, turn_right),
+                lambda at, part: product(get("inverse", at), part),
+            )
+            potential = density
+            for stage in stages:
+                potential = [stage(at, part) for at, part in enumerate(potential)]
         else:
             for at, part in enumerate(density):
                 work_ref[at] = part
@@ -382,14 +379,14 @@
         copy.wait()
 
 
-def hold(*values):
+def hold(*values, flops=0):
     return pl.pallas_call(
         hold_kernel,
         out_shape=[jax.ShapeDtypeStruct(value.shape, value.dtype) for value in values],
         in_specs=[pl.BlockSpec(memory_space=pl.ANY)] * len(values),
         out_specs=[pl.BlockSpec(memory_space=pltpu.VMEM)] * len(values),
         scratch_shapes=[pltpu.SemaphoreType.DMA((len(values),))],
-        cost_estimate=pl.CostEstimate(flops=5 * 10**9, bytes_accessed=2**20, transcendentals=0),
+        cost_estimate=pl.CostEstimate(flops=flops, bytes_accessed=2**16, transcendentals=0),
         compiler_params=pltpu.CompilerParams(vmem_limit_bytes=16 * 2**20),
     )(*values)
 
@@ -424,7 +421,8 @@
     indices = jnp.where(position < stick_count[0], miller, -1).astype(jnp.float32)
     indices = jnp.concatenate([indices, jnp.zeros((6, per_owner), jnp.float32)], axis=0)
     other_indices = rest_of_ring(indices, "pw")
-    own, indices = hold(own, indices)
+    (own,) = hold(own)
+    (indices,) = hold(indices, flops=5 * 10**9)
     indices = [indices] + other_indices
 
     ring = lax.axis_size("band")

time: 22.1 us -> 21.6 us (0.977)
  starting transfers between devices: 8.39 us -> 7.08 us
  waiting for transfers between devices: 1.48 us -> 2.35 us
    ppermute x2, starting transfers between devices: 3.8 us -> 2.04 us  [rest_of_ring(): lax.ppermute(value, axis, [(at, (at + step) % count) for at in range(coun...]
    ppermute x3, waiting for transfers between devices: 1.48 us -> 2.34 us  [swap(): lax.ppermute(value, axis, [(at, partner(at) % count) for at in range(coun...]
    ppermute x3, starting transfers between devices: 4.6 us -> 5.03 us  [swap(): lax.ppermute(value, axis, [(at, partner(at) % count) for at in range(coun...]
    unnamed x4 -> x6, local copies, waits for them, and re-layouts: 0.8 us -> 0.81 us
  transfers between devices with their start and end apart: 5 -> 5, of which waited for: 1 -> 2; matrix products, arithmetic and copies ran while one was open for 3% -> 3% of each run, Pallas kernels for 26% -> 27%
where the time goes in v4:
time: 21.6 us; the launch traced here: 21.4 us
  Pallas kernels  9.65 us (45%)
  starting transfers between devices  7.08 us (33%)
  waiting for transfers between devices  2.35 us (11%)
  local copies, waits for them, and re-layouts  0.83 us (4%)
  between operations  0.77 us (4%)
  other arithmetic  0.72 us (3%)
    pallas_call x3, Pallas kernels, call(): pl.pallas_call(functools.partial(exchange_kernel, batch, points, owners,...  8.65 us
    ppermute x3, starting transfers between devices, swap(): lax.ppermute(value, axis, [(at, partner(at) % count) for at in range(coun...  5.03 us
    ppermute x3, waiting for transfers between devices, swap(): lax.ppermute(value, axis, [(at, partner(at) % count) for at in range(coun...  2.34 us
    ppermute x2, starting transfers between devices, rest_of_ring(): lax.ppermute(value, axis, [(at, (at + step) % count) for at in range(coun...  2.04 us
    pallas_call x1, Pallas kernels, orbitals_of(): pl.pallas_call(functools.partial(orbitals_kernel, count, shapes, where),...  0.94 us
    unnamed x6, local copies, waits for them, and re-layouts  0.81 us
    convert_element_type x1, other arithmetic, shards(): jnp.where(position < stick_count[0], miller, -1).astype(jnp.float32)  0.69 us
  transfers between devices with their start and end apart: 5, of which 2 were waited for; matrix products, arithmetic and copies ran while one was open for 3% of the time, Pallas kernels for 27%

profile of v4, /device:TPU:1, one launch (start us, length us, event | category | flops | bytes accessed | tf_op | source)
XLA Modules:
  0.0 21.4 jit_solution(13934149260812662840)
XLA Ops:
  0.0 2.0 %collective-permute-start.1 = (f32[96,128]{1,0:T(8,128)}, f32[96,128]{1,0:T(8,128)S(1)}, u32[]{:S(2)}, u32[]{:S(2)}) collective-permute-start(f32[96,128]{1,0:T(8,128)} %bitcast.17), channel_id=1, source_target_pairs={{0,16},{16,0},{1,17},{17,1},{2,18},{18,2},{3,19},{19,3},{4,20},{20... | collective-permute-start | bytes 147464 | tf_op jit(solution)/shard_map/ppermute | solution.py:402
  2.7 0.7 %select_convert_fusion = f32[2,128]{1,0:T(2,128)S(1)} fusion(s32[2,128]{1,0:T(2,128)} %param.5, pred[128]{0:T(512)(128)(4,1)S(1)} %iota_compare_fusion), kind=kLoop, calls=%fused_computation.4 | loop fusion | flops 512 | bytes 2176 | tf_op jit(solution)/shard_map/convert_element_type | solution.py:421
  3.4 0.0 collective-permute-start
  3.4 0.0 copy-start
  3.4 0.8 %copy-done = f32[1,2,48,128]{3,2,1,0:T(8,128)S(1)} copy-done((f32[1,2,48,128]{3,2,1,0:T(8,128)S(1)}, f32[1,2,48,128]{3,2,1,0:T(8,128)}, u32[]{:S(2)}) %copy-start) | copy-done | bytes 49176
  4.3 0.0 collective-permute-done.1
  4.3 0.0 slice-start
  4.3 0.0 slice-start.1
  4.3 1.1 %collective-permute-start.2 = (f32[2,96,128]{2,1,0:T(8,128)S(1)}, f32[2,96,128]{2,1,0:T(8,128)S(1)}, u32[]{:S(2)}, u32[]{:S(2)}) collective-permute-start(f32[2,96,128]{2,1,0:T(8,128)S(1)} %get-tuple-element.18.refs_2_), channel_id=1, source_target_pairs={{0,1},{1,0},{2,3},{3,2},{4,5},{5,4},{6,7},{7,6},{8,9},{9,8},{10,11... | collective-permute-start | bytes 294920 | tf_op jit(solution)/shard_map/ppermute | solution.py:396
  5.4 0.9 %collective-permute-done.2.refs_3_ = f32[2,96,128]{2,1,0:T(8,128)S(1)} collective-permute-done((f32[2,96,128]{2,1,0:T(8,128)S(1)}, f32[2,96,128]{2,1,0:T(8,128)S(1)}, u32[]{:S(2)}, u32[]{:S(2)}) %collective-permute-start.2) | collective-permute-done | bytes 98336 | tf_op jit(solution)/shard_map/ppermute | solution.py:396
  6.3 2.1 %collective-permute-start.3 = (f32[2,2,96,128]{3,2,1,0:T(8,128)S(1)}, f32[2,2,96,128]{3,2,1,0:T(8,128)S(1)}, u32[]{:S(2)}, u32[]{:S(2)}) collective-permute-start(f32[2,2,96,128]{3,2,1,0:T(8,128)S(1)} %pad_maximum_fusion), channel_id=1, source_target_pairs={{0,15},{1,2},{2,1},{3,4},{4,3},{5,6},{6,5},{7,8},{8,7},{9,10},{10,... | collective-permute-start | bytes 589832 | tf_op jit(solution)/shard_map/ppermute | solution.py:396
  8.4 0.0 collective-permute-done.refs_1_
  8.4 0.0 slice-done
  8.4 0.0 slice-done.1
  8.4 3.3 %shard_map.48 = (bf16[320,256]{1,0:T(8,128)(2,1)S(1)}, f32[4,368,128]{2,1,0:T(8,128)S(1)}, f32[4,368,128]{2,1,0:T(8,128)S(1)}) custom-call(f32[8,128]{1,0:T(8,128)S(1)} %shard_map.46.refs_0_, f32[8,128]{1,0:T(8,128)S(1)} %collective-permute-done.refs_1_, f32[2,96,128]{2,1,0:T(8,128)S(1)} %get-tuple-element.18.refs_2_, ...), custom_call_target="tpu_custom_call" | custom-call | flops 5000000000 | bytes 4194304 | tf_op jit(solution)/shard_map/pallas_call | solution.py:450
  11.7 1.4 %collective-permute-done.3 = f32[2,2,96,128]{3,2,1,0:T(8,128)S(1)} collective-permute-done((f32[2,2,96,128]{3,2,1,0:T(8,128)S(1)}, f32[2,2,96,128]{3,2,1,0:T(8,128)S(1)}, u32[]{:S(2)}, u32[]{:S(2)}) %collective-permute-start.3) | collective-permute-done | bytes 196640 | tf_op jit(solution)/shard_map/ppermute | solution.py:396
  13.2 0.9 %shard_map.49 = (f32[4,368,128]{2,1,0:T(8,128)S(1)}, f32[4,368,128]{2,1,0:T(8,128)S(1)}) custom-call(bf16[320,256]{1,0:T(8,128)(2,1)S(1)} %get-tuple-element.10.pick_ref.refs_0_, f32[2,96,128]{2,1,0:T(8,128)S(1)} %get-tuple-element.16.refs_0_, f32[2,96,128]{2,1,0:T(8,128)S(1)} %get-tuple-element.15.refs_1_, bf16[3088,1152]{1,0:T(8,128)(2,1)S(1)} %bitcast.14), custom_call_target="tpu_custom_call" | custom-call | flops 1000000000 | bytes 1048576 | tf_op jit(solution)/shard_map/pallas_call | solution.py:464
  14.1 1.9 %collective-permute-start.4 = (f32[4,368,128]{2,1,0:T(8,128)S(1)}, f32[4,368,128]{2,1,0:T(8,128)S(1)}, u32[]{:S(2)}, u32[]{:S(2)}) collective-permute-start(f32[4,368,128]{2,1,0:T(8,128)S(1)} %get-tuple-element.13.refs_3_), channel_id=1, source_target_pairs={{0,1},{1,0},{2,3},{3,2},{4,5},{5,4},{6,7},{7,6},{8,9},{9,8},{10,11... | collective-permute-start | bytes 2261000 | tf_op jit(solution)/shard_map/ppermute | solution.py:396
  16.0 2.4 %shard_map.50.refs_2_ = f32[4,368,128]{2,1,0:T(8,128)S(1)} custom-call(bf16[320,256]{1,0:T(8,128)(2,1)S(1)} %get-tuple-element.10.pick_ref.refs_0_, f32[4,368,128]{2,1,0:T(8,128)S(1)} %get-tuple-element.11.refs_1_, f32[4,368,128]{2,1,0:T(8,128)S(1)} %get-tuple-element.12.refs_2_, f32[4,368,128]{2,1,0:T(8,128)S(1)} %get-tuple-element.13.refs_3_, ...), custom_call_target="tpu_custom_call" | custom-call | flops 5000000000 | bytes 4194304 | tf_op jit(solution)/shard_map/pallas_call | solution.py:450
  18.4 0.0 collective-permute-done.4.refs_3_
  18.4 3.0 %shard_map.51 = f32[96,128]{1,0:T(8,128)} custom-call(bf16[320,256]{1,0:T(8,128)(2,1)S(1)} %get-tuple-element.10.pick_ref.refs_0_, f32[4,368,128]{2,1,0:T(8,128)S(1)} %get-tuple-element.11.refs_1_, f32[4,368,128]{2,1,0:T(8,128)S(1)} %shard_map.50.refs_2_, f32[4,368,128]{2,1,0:T(8,128)S(1)} %collective-permute-done.4.refs_3_, bf16[3088,1152]{1,0:T(8,128)(2,1)S(1)} %bitcast.14), custom_call_target="tpu_custom_call" | custom-call | flops 5000000000 | bytes 4194304 | tf_op jit(solution)/shard_map/pallas_call | solution.py:450
  (8 shorter events, 0.1 us)
Async XLA Ops:
  0.0 4.3 %collective-permute-start.1 = (f32[96,128]{1,0:T(8,128)}, f32[96,128]{1,0:T(8,128)S(1)}, u32[]{:S(2)}, u32[]{:S(2)}) collective-permute-start(f32[96,128]{1,0:T(8,128)} %bitcast.17), channel_id=1, source_target_pairs={{0,16},{16,0},{1,17},{17,1},{2,18},{18,2},{3,19},{19,3},{4,20},{20... | collective-permute-start | bytes 147464 | tf_op jit(solution)/shard_map/ppermute | solution.py:402
  3.4 5.0 %collective-permute-start = (f32[8,128]{1,0:T(8,128)S(1)}, f32[8,128]{1,0:T(8,128)S(1)}, u32[]{:S(2)}, u32[]{:S(2)}) collective-permute-start(f32[8,128]{1,0:T(8,128)S(1)} %concatenate.3.refs_0_), channel_id=1, source_target_pairs={{0,16},{16,0},{1,17},{17,1},{2,18},{18,2},{3,19},{19,3},{4,20},{20... | collective-permute-start | bytes 12296 | tf_op jit(solution)/shard_map/ppermute | solution.py:402
  3.4 0.8 %copy-start = (f32[1,2,48,128]{3,2,1,0:T(8,128)S(1)}, f32[1,2,48,128]{3,2,1,0:T(8,128)}, u32[]{:S(2)}) copy-start(f32[1,2,48,128]{3,2,1,0:T(8,128)} %param.4) | copy-start | bytes 147460
  4.3 4.1 %slice-start = ((s8[7114752]{0:T(1024)(128)(4,1)}), s8[4194304]{0:T(1024)(128)(4,1)S(1)}, s32[]{:S(2)}) async-start(s8[7114752]{0:T(1024)(128)(4,1)} %bitcast.13), calls=%async_computation | async-start | bytes 8388608
  4.3 4.1 %slice-start.1 = ((s8[7114752]{0:T(1024)(128)(4,1)}), s8[2920448]{0:T(1024)(128)(4,1)S(1)}, s32[]{:S(2)}) async-start(s8[7114752]{0:T(1024)(128)(4,1)} %bitcast.13), calls=%async_computation.1 | async-start | bytes 5840896
  4.3 2.0 %collective-permute-start.2 = (f32[2,96,128]{2,1,0:T(8,128)S(1)}, f32[2,96,128]{2,1,0:T(8,128)S(1)}, u32[]{:S(2)}, u32[]{:S(2)}) collective-permute-start(f32[2,96,128]{2,1,0:T(8,128)S(1)} %get-tuple-element.18.refs_2_), channel_id=1, source_target_pairs={{0,1},{1,0},{2,3},{3,2},{4,5},{5,4},{6,7},{7,6},{8,9},{9,8},{10,11... | collective-permute-start | bytes 294920 | tf_op jit(solution)/shard_map/ppermute | solution.py:396
  6.3 6.8 %collective-permute-start.3 = (f32[2,2,96,128]{3,2,1,0:T(8,128)S(1)}, f32[2,2,96,128]{3,2,1,0:T(8,128)S(1)}, u32[]{:S(2)}, u32[]{:S(2)}) collective-permute-start(f32[2,2,96,128]{3,2,1,0:T(8,128)S(1)} %pad_maximum_fusion), channel_id=1, source_target_pairs={{0,15},{1,2},{2,1},{3,4},{4,3},{5,6},{6,5},{7,8},{8,7},{9,10},{10,... | collective-permute-start | bytes 589832 | tf_op jit(solution)/shard_map/ppermute | solution.py:396
  14.1 4.3 %collective-permute-start.4 = (f32[4,368,128]{2,1,0:T(8,128)S(1)}, f32[4,368,128]{2,1,0:T(8,128)S(1)}, u32[]{:S(2)}, u32[]{:S(2)}) collective-permute-start(f32[4,368,128]{2,1,0:T(8,128)S(1)} %get-tuple-element.13.refs_3_), channel_id=1, source_target_pairs={{0,1},{1,0},{2,3},{3,2},{4,5},{5,4},{6,7},{7,6},{8,9},{9,8},{10,11... | collective-permute-start | bytes 2261000 | tf_op jit(solution)/shard_map/ppermute | solution.py:396

commit v5 on v4

--- a/solution.py
+++ b/solution.py
@@ -82,7 +82,7 @@
         full = np.zeros((rows, cols))
         full[: table.shape[0], : table.shape[1]] = table
         high, low = split_table(full)
-        return np.concatenate([high, high, low], axis=1)
+        return np.concatenate([high, low, high], axis=1)
 
     n_place = round_up(len(place), ROWS)
     n_pairs = round_up(len(pairs), ROWS)
@@ -111,7 +111,7 @@
         at = member * points
         block[at : at + points, at : at + points] = cas
     high, low = split_table(block)
-    turn_left = np.concatenate([high, high, low], axis=1)
+    turn_left = np.concatenate([high, low, high], axis=1)
     turn_right = np.block([[high, low], [high, low]])
 
     squares = signed.astype(np.float64) ** 2
@@ -188,16 +188,16 @@
 
 def stacked(value):
     high, low = split(value)
-    return jnp.concatenate([high, low, high], axis=0)
+    return jnp.concatenate([high, high, low], axis=0)
 
 
 def product(table, value):
     depth, lanes = value.shape
     if lanes > LANES or depth <= LANES:
         return dot(table, stacked(value))
-    high, low = split(value)
-    out = dot(table[:, :depth], jnp.concatenate([high, low], axis=1))
-    return out[:, :lanes] + out[:, lanes:] + dot(table[:, 2 * depth :], high)
+    halves = jnp.concatenate(split(value), axis=1)
+    out = dot(table[:, : 2 * depth], jnp.concatenate([halves, halves], axis=0))
+    return out[:, :lanes] + out[:, lanes:]
 
 
 def pick_matrix(indices, codes, points):

time: 21.6 us -> 21.5 us (level)
  no operation moved by 1% of the time
where the time goes in v5:
time: 21.5 us; the launch traced here: 21.3 us
  Pallas kernels  9.59 us (45%)
  starting transfers between devices  7.08 us (33%)
  waiting for transfers between devices  2.34 us (11%)
  local copies, waits for them, and re-layouts  0.83 us (4%)
  between operations  0.77 us (4%)
  other arithmetic  0.72 us (3%)
    pallas_call x3, Pallas kernels, call(): pl.pallas_call(functools.partial(exchange_kernel, batch, points, owners,...  8.61 us
    ppermute x3, starting transfers between devices, swap(): lax.ppermute(value, axis, [(at, partner(at) % count) for at in range(coun...  5.04 us
    ppermute x3, waiting for transfers between devices, swap(): lax.ppermute(value, axis, [(at, partner(at) % count) for at in range(coun...  2.33 us
    ppermute x2, starting transfers between devices, rest_of_ring(): lax.ppermute(value, axis, [(at, (at + step) % count) for at in range(coun...  2.04 us
    pallas_call x1, Pallas kernels, orbitals_of(): pl.pallas_call(functools.partial(orbitals_kernel, count, shapes, where),...  0.93 us
    unnamed x6, local copies, waits for them, and re-layouts  0.81 us
    convert_element_type x1, other arithmetic, shards(): jnp.where(position < stick_count[0], miller, -1).astype(jnp.float32)  0.69 us
  transfers between devices with their start and end apart: 5, of which 2 were waited for; matrix products, arithmetic and copies ran while one was open for 3% of the time, Pallas kernels for 27%

profile of v5, /device:TPU:1, one launch (start us, length us, event | category | flops | bytes accessed | tf_op | source)
XLA Modules:
  0.0 21.3 jit_solution(12900263626521391444)
XLA Ops:
  0.0 2.0 %collective-permute-start.1 = (f32[96,128]{1,0:T(8,128)}, f32[96,128]{1,0:T(8,128)S(1)}, u32[]{:S(2)}, u32[]{:S(2)}) collective-permute-start(f32[96,128]{1,0:T(8,128)} %bitcast.17), channel_id=1, source_target_pairs={{0,16},{16,0},{1,17},{17,1},{2,18},{18,2},{3,19},{19,3},{4,20},{20... | collective-permute-start | bytes 147464 | tf_op jit(solution)/shard_map/ppermute | solution.py:402
  2.7 0.7 %select_convert_fusion = f32[2,128]{1,0:T(2,128)S(1)} fusion(s32[2,128]{1,0:T(2,128)} %param.5, pred[128]{0:T(512)(128)(4,1)S(1)} %iota_compare_fusion), kind=kLoop, calls=%fused_computation.4 | loop fusion | flops 512 | bytes 2176 | tf_op jit(solution)/shard_map/convert_element_type | solution.py:421
  3.4 0.0 collective-permute-start
  3.4 0.0 copy-start
  3.4 0.8 %copy-done = f32[1,2,48,128]{3,2,1,0:T(8,128)S(1)} copy-done((f32[1,2,48,128]{3,2,1,0:T(8,128)S(1)}, f32[1,2,48,128]{3,2,1,0:T(8,128)}, u32[]{:S(2)}) %copy-start) | copy-done | bytes 49176
  4.3 0.0 collective-permute-done.1
  4.3 0.0 slice-start
  4.3 0.0 slice-start.1
  4.3 1.1 %collective-permute-start.2 = (f32[2,96,128]{2,1,0:T(8,128)S(1)}, f32[2,96,128]{2,1,0:T(8,128)S(1)}, u32[]{:S(2)}, u32[]{:S(2)}) collective-permute-start(f32[2,96,128]{2,1,0:T(8,128)S(1)} %get-tuple-element.18.refs_2_), channel_id=1, source_target_pairs={{0,1},{1,0},{2,3},{3,2},{4,5},{5,4},{6,7},{7,6},{8,9},{9,8},{10,11... | collective-permute-start | bytes 294920 | tf_op jit(solution)/shard_map/ppermute | solution.py:396
  5.4 0.9 %collective-permute-done.2.refs_3_ = f32[2,96,128]{2,1,0:T(8,128)S(1)} collective-permute-done((f32[2,96,128]{2,1,0:T(8,128)S(1)}, f32[2,96,128]{2,1,0:T(8,128)S(1)}, u32[]{:S(2)}, u32[]{:S(2)}) %collective-permute-start.2) | collective-permute-done | bytes 98336 | tf_op jit(solution)/shard_map/ppermute | solution.py:396
  6.3 2.1 %collective-permute-start.3 = (f32[2,2,96,128]{3,2,1,0:T(8,128)S(1)}, f32[2,2,96,128]{3,2,1,0:T(8,128)S(1)}, u32[]{:S(2)}, u32[]{:S(2)}) collective-permute-start(f32[2,2,96,128]{3,2,1,0:T(8,128)S(1)} %pad_maximum_fusion), channel_id=1, source_target_pairs={{0,15},{1,2},{2,1},{3,4},{4,3},{5,6},{6,5},{7,8},{8,7},{9,10},{10,... | collective-permute-start | bytes 589832 | tf_op jit(solution)/shard_map/ppermute | solution.py:396
  8.4 0.0 collective-permute-done.refs_1_
  8.4 0.0 slice-done
  8.4 0.0 slice-done.1
  8.4 3.3 %shard_map.48 = (bf16[320,256]{1,0:T(8,128)(2,1)S(1)}, f32[4,368,128]{2,1,0:T(8,128)S(1)}, f32[4,368,128]{2,1,0:T(8,128)S(1)}) custom-call(f32[8,128]{1,0:T(8,128)S(1)} %shard_map.46.refs_0_, f32[8,128]{1,0:T(8,128)S(1)} %collective-permute-done.refs_1_, f32[2,96,128]{2,1,0:T(8,128)S(1)} %get-tuple-element.18.refs_2_, ...), custom_call_target="tpu_custom_call" | custom-call | flops 5000000000 | bytes 4194304 | tf_op jit(solution)/shard_map/pallas_call | solution.py:450
  11.7 1.4 %collective-permute-done.3 = f32[2,2,96,128]{3,2,1,0:T(8,128)S(1)} collective-permute-done((f32[2,2,96,128]{3,2,1,0:T(8,128)S(1)}, f32[2,2,96,128]{3,2,1,0:T(8,128)S(1)}, u32[]{:S(2)}, u32[]{:S(2)}) %collective-permute-start.3) | collective-permute-done | bytes 196640 | tf_op jit(solution)/shard_map/ppermute | solution.py:396
  13.2 0.9 %shard_map.49 = (f32[4,368,128]{2,1,0:T(8,128)S(1)}, f32[4,368,128]{2,1,0:T(8,128)S(1)}) custom-call(bf16[320,256]{1,0:T(8,128)(2,1)S(1)} %get-tuple-element.10.pick_ref.refs_0_, f32[2,96,128]{2,1,0:T(8,128)S(1)} %get-tuple-element.16.refs_0_, f32[2,96,128]{2,1,0:T(8,128)S(1)} %get-tuple-element.15.refs_1_, bf16[3088,1152]{1,0:T(8,128)(2,1)S(1)} %bitcast.14), custom_call_target="tpu_custom_call" | custom-call | flops 1000000000 | bytes 1048576 | tf_op jit(solution)/shard_map/pallas_call | solution.py:464
  14.1 1.9 %collective-permute-start.4 = (f32[4,368,128]{2,1,0:T(8,128)S(1)}, f32[4,368,128]{2,1,0:T(8,128)S(1)}, u32[]{:S(2)}, u32[]{:S(2)}) collective-permute-start(f32[4,368,128]{2,1,0:T(8,128)S(1)} %get-tuple-element.13.refs_3_), channel_id=1, source_target_pairs={{0,1},{1,0},{2,3},{3,2},{4,5},{5,4},{6,7},{7,6},{8,9},{9,8},{10,11... | collective-permute-start | bytes 2261000 | tf_op jit(solution)/shard_map/ppermute | solution.py:396
  16.0 2.4 %shard_map.50.refs_2_ = f32[4,368,128]{2,1,0:T(8,128)S(1)} custom-call(bf16[320,256]{1,0:T(8,128)(2,1)S(1)} %get-tuple-element.10.pick_ref.refs_0_, f32[4,368,128]{2,1,0:T(8,128)S(1)} %get-tuple-element.11.refs_1_, f32[4,368,128]{2,1,0:T(8,128)S(1)} %get-tuple-element.12.refs_2_, f32[4,368,128]{2,1,0:T(8,128)S(1)} %get-tuple-element.13.refs_3_, ...), custom_call_target="tpu_custom_call" | custom-call | flops 5000000000 | bytes 4194304 | tf_op jit(solution)/shard_map/pallas_call | solution.py:450
  18.4 0.0 collective-permute-done.4.refs_3_
  18.4 2.9 %shard_map.51 = f32[96,128]{1,0:T(8,128)} custom-call(bf16[320,256]{1,0:T(8,128)(2,1)S(1)} %get-tuple-element.10.pick_ref.refs_0_, f32[4,368,128]{2,1,0:T(8,128)S(1)} %get-tuple-element.11.refs_1_, f32[4,368,128]{2,1,0:T(8,128)S(1)} %shard_map.50.refs_2_, f32[4,368,128]{2,1,0:T(8,128)S(1)} %collective-permute-done.4.refs_3_, bf16[3088,1152]{1,0:T(8,128)(2,1)S(1)} %bitcast.14), custom_call_target="tpu_custom_call" | custom-call | flops 5000000000 | bytes 4194304 | tf_op jit(solution)/shard_map/pallas_call | solution.py:450
  (8 shorter events, 0.1 us)
Async XLA Ops:
  0.0 4.3 %collective-permute-start.1 = (f32[96,128]{1,0:T(8,128)}, f32[96,128]{1,0:T(8,128)S(1)}, u32[]{:S(2)}, u32[]{:S(2)}) collective-permute-start(f32[96,128]{1,0:T(8,128)} %bitcast.17), channel_id=1, source_target_pairs={{0,16},{16,0},{1,17},{17,1},{2,18},{18,2},{3,19},{19,3},{4,20},{20... | collective-permute-start | bytes 147464 | tf_op jit(solution)/shard_map/ppermute | solution.py:402
  3.4 5.0 %collective-permute-start = (f32[8,128]{1,0:T(8,128)S(1)}, f32[8,128]{1,0:T(8,128)S(1)}, u32[]{:S(2)}, u32[]{:S(2)}) collective-permute-start(f32[8,128]{1,0:T(8,128)S(1)} %concatenate.3.refs_0_), channel_id=1, source_target_pairs={{0,16},{16,0},{1,17},{17,1},{2,18},{18,2},{3,19},{19,3},{4,20},{20... | collective-permute-start | bytes 12296 | tf_op jit(solution)/shard_map/ppermute | solution.py:402
  3.4 0.8 %copy-start = (f32[1,2,48,128]{3,2,1,0:T(8,128)S(1)}, f32[1,2,48,128]{3,2,1,0:T(8,128)}, u32[]{:S(2)}) copy-start(f32[1,2,48,128]{3,2,1,0:T(8,128)} %param.4) | copy-start | bytes 147460
  4.3 4.1 %slice-start = ((s8[7114752]{0:T(1024)(128)(4,1)}), s8[4194304]{0:T(1024)(128)(4,1)S(1)}, s32[]{:S(2)}) async-start(s8[7114752]{0:T(1024)(128)(4,1)} %bitcast.13), calls=%async_computation | async-start | bytes 8388608
  4.3 4.1 %slice-start.1 = ((s8[7114752]{0:T(1024)(128)(4,1)}), s8[2920448]{0:T(1024)(128)(4,1)S(1)}, s32[]{:S(2)}) async-start(s8[7114752]{0:T(1024)(128)(4,1)} %bitcast.13), calls=%async_computation.1 | async-start | bytes 5840896
  4.3 2.0 %collective-permute-start.2 = (f32[2,96,128]{2,1,0:T(8,128)S(1)}, f32[2,96,128]{2,1,0:T(8,128)S(1)}, u32[]{:S(2)}, u32[]{:S(2)}) collective-permute-start(f32[2,96,128]{2,1,0:T(8,128)S(1)} %get-tuple-element.18.refs_2_), channel_id=1, source_target_pairs={{0,1},{1,0},{2,3},{3,2},{4,5},{5,4},{6,7},{7,6},{8,9},{9,8},{10,11... | collective-permute-start | bytes 294920 | tf_op jit(solution)/shard_map/ppermute | solution.py:396
  6.3 6.8 %collective-permute-start.3 = (f32[2,2,96,128]{3,2,1,0:T(8,128)S(1)}, f32[2,2,96,128]{3,2,1,0:T(8,128)S(1)}, u32[]{:S(2)}, u32[]{:S(2)}) collective-permute-start(f32[2,2,96,128]{3,2,1,0:T(8,128)S(1)} %pad_maximum_fusion), channel_id=1, source_target_pairs={{0,15},{1,2},{2,1},{3,4},{4,3},{5,6},{6,5},{7,8},{8,7},{9,10},{10,... | collective-permute-start | bytes 589832 | tf_op jit(solution)/shard_map/ppermute | solution.py:396
  14.1 4.3 %collective-permute-start.4 = (f32[4,368,128]{2,1,0:T(8,128)S(1)}, f32[4,368,128]{2,1,0:T(8,128)S(1)}, u32[]{:S(2)}, u32[]{:S(2)}) collective-permute-start(f32[4,368,128]{2,1,0:T(8,128)S(1)} %get-tuple-element.13.refs_3_), channel_id=1, source_target_pairs={{0,1},{1,0},{2,3},{3,2},{4,5},{5,4},{6,7},{7,6},{8,9},{9,8},{10,11... | collective-permute-start | bytes 2261000 | tf_op jit(solution)/shard_map/ppermute | solution.py:396

commit v6 on v5

--- a/solution.py
+++ b/solution.py
@@ -417,6 +417,7 @@
     values = [jnp.asarray(table) for table in held]
     own = stick_coefs.reshape(members * points, per_owner)
     others = rest_of_ring(own, "pw")
+    early = swap(own, "band", lambda at: at ^ 1)
     position = jnp.arange(per_owner, dtype=jnp.int32)[None]
     indices = jnp.where(position < stick_count[0], miller, -1).astype(jnp.float32)
     indices = jnp.concatenate([indices, jnp.zeros((6, per_owner), jnp.float32)], axis=0)
@@ -427,7 +428,7 @@
 
     ring = lax.axis_size("band")
     coefs = jnp.stack([own] + others)
-    mate = swap(coefs, "band", lambda at: at ^ 1)
+    mate = jnp.stack([early] + [swap(other, "band", lambda at: at ^ 1) for other in others])
     got = swap(jnp.stack([coefs, mate]), "band", lambda at: at + 1 if at & 1 else at - 1 + ring)
 
     lanes = tables["turn_right"].shape[0] // 2

time: 21.5 us -> 21.4 us (level)
    ppermute x3 -> x4, starting transfers between devices: 5.04 us -> 4.28 us  [swap(): lax.ppermute(value, axis, [(at, partner(at) % count) for at in range(coun...]
    ppermute x2, starting transfers between devices: 2.04 us -> 2.73 us  [rest_of_ring(): lax.ppermute(value, axis, [(at, (at + step) % count) for at in range(coun...]
    ppermute x3 -> x4, waiting for transfers between devices: 2.33 us -> 2.27 us  [swap(): lax.ppermute(value, axis, [(at, partner(at) % count) for at in range(coun...]
  transfers between devices with their start and end apart: 5 -> 6, of which waited for: 2 -> 2; matrix products, arithmetic and copies ran while one was open for 3% -> 3% of each run, Pallas kernels for 27% -> 27%
where the time goes in v6:
time: 21.4 us; the launch traced here: 21.3 us
  Pallas kernels  9.6 us (45%)
  starting transfers between devices  7.01 us (33%)
  waiting for transfers between devices  2.28 us (11%)
  local copies, waits for them, and re-layouts  0.86 us (4%)
  between operations  0.78 us (4%)
  other arithmetic  0.74 us (3%)
    pallas_call x3, Pallas kernels, call(): pl.pallas_call(functools.partial(exchange_kernel, batch, points, owners,...  8.61 us
    ppermute x4, starting transfers between devices, swap(): lax.ppermute(value, axis, [(at, partner(at) % count) for at in range(coun...  4.28 us
    ppermute x2, starting transfers between devices, rest_of_ring(): lax.ppermute(value, axis, [(at, (at + step) % count) for at in range(coun...  2.73 us
    ppermute x4, waiting for transfers between devices, swap(): lax.ppermute(value, axis, [(at, partner(at) % count) for at in range(coun...  2.27 us
    pallas_call x1, Pallas kernels, orbitals_of(): pl.pallas_call(functools.partial(orbitals_kernel, count, shapes, where),...  0.94 us
    unnamed x6, local copies, waits for them, and re-layouts  0.84 us
    convert_element_type x1, other arithmetic, shards(): jnp.where(position < stick_count[0], miller, -1).astype(jnp.float32)  0.69 us
  transfers between devices with their start and end apart: 6, of which 2 were waited for; matrix products, arithmetic and copies ran while one was open for 3% of the time, Pallas kernels for 27%

profile of v6, /device:TPU:1, one launch (start us, length us, event | category | flops | bytes accessed | tf_op | source)
XLA Modules:
  0.0 21.3 jit_solution(12374708668154614871)
XLA Ops:
  0.0 0.1 collective-permute-start.2
  0.1 2.7 %collective-permute-start.1 = (f32[96,128]{1,0:T(8,128)}, f32[96,128]{1,0:T(8,128)S(1)}, u32[]{:S(2)}, u32[]{:S(2)}) collective-permute-start(f32[96,128]{1,0:T(8,128)} %bitcast.20), channel_id=1, source_target_pairs={{0,16},{16,0},{1,17},{17,1},{2,18},{18,2},{3,19},{19,3},{4,20},{20... | collective-permute-start | bytes 147464 | tf_op jit(solution)/shard_map/ppermute | solution.py:402
  3.4 0.7 %select_convert_fusion = f32[2,128]{1,0:T(2,128)S(1)} fusion(s32[2,128]{1,0:T(2,128)} %param.5, pred[128]{0:T(512)(128)(4,1)S(1)} %iota_compare_fusion), kind=kLoop, calls=%fused_computation.5 | loop fusion | flops 512 | bytes 2176 | tf_op jit(solution)/shard_map/convert_element_type | solution.py:422
  4.1 0.0 slice-start
  4.1 0.0 copy-start
  4.1 0.0 slice-start.1
  4.1 0.1 collective-permute-start
  4.2 0.8 %copy-done = f32[1,2,48,128]{3,2,1,0:T(8,128)S(1)} copy-done((f32[1,2,48,128]{3,2,1,0:T(8,128)S(1)}, f32[1,2,48,128]{3,2,1,0:T(8,128)}, u32[]{:S(2)}) %copy-start) | copy-done | bytes 49176
  5.1 0.0 collective-permute-done.1
  5.1 0.5 %collective-permute-start.3 = (f32[96,128]{1,0:T(8,128)S(1)}, f32[96,128]{1,0:T(8,128)S(1)}, u32[]{:S(2)}, u32[]{:S(2)}) collective-permute-start(f32[96,128]{1,0:T(8,128)S(1)} %collective-permute-done.1), channel_id=1, source_target_pairs={{0,1},{1,0},{2,3},{3,2},{4,5},{5,4},{6,7},{7,6},{8,9},{9,8},{10,11... | collective-permute-start | bytes 147464 | tf_op jit(solution)/shard_map/ppermute | solution.py:396
  5.6 0.0 collective-permute-done.2
  5.6 0.9 %collective-permute-done.3 = f32[96,128]{1,0:T(8,128)S(1)} collective-permute-done((f32[96,128]{1,0:T(8,128)S(1)}, f32[96,128]{1,0:T(8,128)S(1)}, u32[]{:S(2)}, u32[]{:S(2)}) %collective-permute-start.3) | collective-permute-done | bytes 49184 | tf_op jit(solution)/shard_map/ppermute | solution.py:396
  6.5 1.8 %collective-permute-start.4 = (f32[2,2,96,128]{3,2,1,0:T(8,128)S(1)}, f32[2,2,96,128]{3,2,1,0:T(8,128)S(1)}, u32[]{:S(2)}, u32[]{:S(2)}) collective-permute-start(f32[2,2,96,128]{3,2,1,0:T(8,128)S(1)} %pad_maximum_fusion), channel_id=1, source_target_pairs={{0,15},{1,2},{2,1},{3,4},{4,3},{5,6},{6,5},{7,8},{8,7},{9,10},{10,... | collective-permute-start | bytes 589832 | tf_op jit(solution)/shard_map/ppermute | solution.py:396
  8.3 0.0 collective-permute-done.refs_1_
  8.3 0.0 slice-done
  8.3 0.0 slice-done.1
  8.4 3.3 %shard_map.48 = (bf16[320,256]{1,0:T(8,128)(2,1)S(1)}, f32[4,368,128]{2,1,0:T(8,128)S(1)}, f32[4,368,128]{2,1,0:T(8,128)S(1)}) custom-call(f32[8,128]{1,0:T(8,128)S(1)} %shard_map.46.refs_0_, f32[8,128]{1,0:T(8,128)S(1)} %collective-permute-done.refs_1_, f32[2,96,128]{2,1,0:T(8,128)S(1)} %get-tuple-element.18.refs_2_, ...), custom_call_target="tpu_custom_call" | custom-call | flops 5000000000 | bytes 4194304 | tf_op jit(solution)/shard_map/pallas_call | solution.py:451
  11.6 1.4 %collective-permute-done.4 = f32[2,2,96,128]{3,2,1,0:T(8,128)S(1)} collective-permute-done((f32[2,2,96,128]{3,2,1,0:T(8,128)S(1)}, f32[2,2,96,128]{3,2,1,0:T(8,128)S(1)}, u32[]{:S(2)}, u32[]{:S(2)}) %collective-permute-start.4) | collective-permute-done | bytes 196640 | tf_op jit(solution)/shard_map/ppermute | solution.py:396
  13.1 0.9 %shard_map.49 = (f32[4,368,128]{2,1,0:T(8,128)S(1)}, f32[4,368,128]{2,1,0:T(8,128)S(1)}) custom-call(bf16[320,256]{1,0:T(8,128)(2,1)S(1)} %get-tuple-element.10.pick_ref.refs_0_, f32[2,96,128]{2,1,0:T(8,128)S(1)} %get-tuple-element.16.refs_0_, f32[2,96,128]{2,1,0:T(8,128)S(1)} %get-tuple-element.15.refs_1_, bf16[3088,1152]{1,0:T(8,128)(2,1)S(1)} %bitcast.17), custom_call_target="tpu_custom_call" | custom-call | flops 1000000000 | bytes 1048576 | tf_op jit(solution)/shard_map/pallas_call | solution.py:465
  14.0 1.9 %collective-permute-start.5 = (f32[4,368,128]{2,1,0:T(8,128)S(1)}, f32[4,368,128]{2,1,0:T(8,128)S(1)}, u32[]{:S(2)}, u32[]{:S(2)}) collective-permute-start(f32[4,368,128]{2,1,0:T(8,128)S(1)} %get-tuple-element.13.refs_3_), channel_id=1, source_target_pairs={{0,1},{1,0},{2,3},{3,2},{4,5},{5,4},{6,7},{7,6},{8,9},{9,8},{10,11... | collective-permute-start | bytes 2261000 | tf_op jit(solution)/shard_map/ppermute | solution.py:396
  15.9 2.4 %shard_map.50.refs_2_ = f32[4,368,128]{2,1,0:T(8,128)S(1)} custom-call(bf16[320,256]{1,0:T(8,128)(2,1)S(1)} %get-tuple-element.10.pick_ref.refs_0_, f32[4,368,128]{2,1,0:T(8,128)S(1)} %get-tuple-element.11.refs_1_, f32[4,368,128]{2,1,0:T(8,128)S(1)} %get-tuple-element.12.refs_2_, f32[4,368,128]{2,1,0:T(8,128)S(1)} %get-tuple-element.13.refs_3_, ...), custom_call_target="tpu_custom_call" | custom-call | flops 5000000000 | bytes 4194304 | tf_op jit(solution)/shard_map/pallas_call | solution.py:451
  18.3 0.0 collective-permute-done.5.refs_3_
  18.4 2.9 %shard_map.51 = f32[96,128]{1,0:T(8,128)} custom-call(bf16[320,256]{1,0:T(8,128)(2,1)S(1)} %get-tuple-element.10.pick_ref.refs_0_, f32[4,368,128]{2,1,0:T(8,128)S(1)} %get-tuple-element.11.refs_1_, f32[4,368,128]{2,1,0:T(8,128)S(1)} %shard_map.50.refs_2_, f32[4,368,128]{2,1,0:T(8,128)S(1)} %collective-permute-done.5.refs_3_, bf16[3088,1152]{1,0:T(8,128)(2,1)S(1)} %bitcast.17), custom_call_target="tpu_custom_call" | custom-call | flops 5000000000 | bytes 4194304 | tf_op jit(solution)/shard_map/pallas_call | solution.py:451
  (9 shorter events, 0.1 us)
Async XLA Ops:
  0.0 5.6 %collective-permute-start.2 = (f32[96,128]{1,0:T(8,128)}, f32[96,128]{1,0:T(8,128)S(1)}, u32[]{:S(2)}, u32[]{:S(2)}) collective-permute-start(f32[96,128]{1,0:T(8,128)} %bitcast.19), channel_id=1, source_target_pairs={{0,1},{1,0},{2,3},{3,2},{4,5},{5,4},{6,7},{7,6},{8,9},{9,8},{10,11... | collective-permute-start | bytes 147464 | tf_op jit(solution)/shard_map/ppermute | solution.py:396
  0.1 5.0 %collective-permute-start.1 = (f32[96,128]{1,0:T(8,128)}, f32[96,128]{1,0:T(8,128)S(1)}, u32[]{:S(2)}, u32[]{:S(2)}) collective-permute-start(f32[96,128]{1,0:T(8,128)} %bitcast.20), channel_id=1, source_target_pairs={{0,16},{16,0},{1,17},{17,1},{2,18},{18,2},{3,19},{19,3},{4,20},{20... | collective-permute-start | bytes 147464 | tf_op jit(solution)/shard_map/ppermute | solution.py:402
  4.1 4.3 %slice-start = ((s8[7114752]{0:T(1024)(128)(4,1)}), s8[4194304]{0:T(1024)(128)(4,1)S(1)}, s32[]{:S(2)}) async-start(s8[7114752]{0:T(1024)(128)(4,1)} %bitcast.16), calls=%async_computation | async-start | bytes 8388608
  4.1 1.0 %copy-start = (f32[1,2,48,128]{3,2,1,0:T(8,128)S(1)}, f32[1,2,48,128]{3,2,1,0:T(8,128)}, u32[]{:S(2)}) copy-start(f32[1,2,48,128]{3,2,1,0:T(8,128)} %param.4) | copy-start | bytes 147460
  4.1 4.3 %slice-start.1 = ((s8[7114752]{0:T(1024)(128)(4,1)}), s8[2920448]{0:T(1024)(128)(4,1)S(1)}, s32[]{:S(2)}) async-start(s8[7114752]{0:T(1024)(128)(4,1)} %bitcast.16), calls=%async_computation.1 | async-start | bytes 5840896
  4.1 4.2 %collective-permute-start = (f32[8,128]{1,0:T(8,128)S(1)}, f32[8,128]{1,0:T(8,128)S(1)}, u32[]{:S(2)}, u32[]{:S(2)}) collective-permute-start(f32[8,128]{1,0:T(8,128)S(1)} %concatenate.3.refs_0_), channel_id=1, source_target_pairs={{0,16},{16,0},{1,17},{17,1},{2,18},{18,2},{3,19},{19,3},{4,20},{20... | collective-permute-start | bytes 12296 | tf_op jit(solution)/shard_map/ppermute | solution.py:402
  5.1 1.4 %collective-permute-start.3 = (f32[96,128]{1,0:T(8,128)S(1)}, f32[96,128]{1,0:T(8,128)S(1)}, u32[]{:S(2)}, u32[]{:S(2)}) collective-permute-start(f32[96,128]{1,0:T(8,128)S(1)} %collective-permute-done.1), channel_id=1, source_target_pairs={{0,1},{1,0},{2,3},{3,2},{4,5},{5,4},{6,7},{7,6},{8,9},{9,8},{10,11... | collective-permute-start | bytes 147464 | tf_op jit(solution)/shard_map/ppermute | solution.py:396
  6.5 6.5 %collective-permute-start.4 = (f32[2,2,96,128]{3,2,1,0:T(8,128)S(1)}, f32[2,2,96,128]{3,2,1,0:T(8,128)S(1)}, u32[]{:S(2)}, u32[]{:S(2)}) collective-permute-start(f32[2,2,96,128]{3,2,1,0:T(8,128)S(1)} %pad_maximum_fusion), channel_id=1, source_target_pairs={{0,15},{1,2},{2,1},{3,4},{4,3},{5,6},{6,5},{7,8},{8,7},{9,10},{10,... | collective-permute-start | bytes 589832 | tf_op jit(solution)/shard_map/ppermute | solution.py:396
  14.0 4.3 %collective-permute-start.5 = (f32[4,368,128]{2,1,0:T(8,128)S(1)}, f32[4,368,128]{2,1,0:T(8,128)S(1)}, u32[]{:S(2)}, u32[]{:S(2)}) collective-permute-start(f32[4,368,128]{2,1,0:T(8,128)S(1)} %get-tuple-element.13.refs_3_), channel_id=1, source_target_pairs={{0,1},{1,0},{2,3},{3,2},{4,5},{5,4},{6,7},{7,6},{8,9},{9,8},{10,11... | collective-permute-start | bytes 2261000 | tf_op jit(solution)/shard_map/ppermute | solution.py:396

commit v7 on v6

--- a/solution.py
+++ b/solution.py
@@ -293,6 +293,8 @@
     else:
         (field_ref,) = take(1)
     visit_all_ref, work_all_ref, coefs_all_ref = take(3)
+    if ends and ready:
+        held_ref, semaphores = take(2)
     if begins and ends:
         pick_ref, own_ref, field_ref = take(3)
     if begins:
@@ -363,8 +365,19 @@
         coefs = turn(jnp.concatenate(coefs, axis=0), turn_right)
         high, low = split(coefs.T)
         own_pick = pick[:, : out_ref.shape[1]]
-        result = dot(high, own_pick) + dot(low, own_pick)
-        out_ref[...] = result[: members * points]
+        if not ready:
+            out_ref[...] = (dot(high, own_pick) + dot(low, own_pick))[: members * points]
+            return
+        copies = []
+        for member in range(members):
+            here = slice(member * points, (member + 1) * points)
+            held_ref[here] = dot(high[here], own_pick) + dot(low[here], own_pick)
+            copies.append(
+                pltpu.make_async_copy(held_ref.at[here], out_ref.at[here], semaphores.at[member])
+            )
+            copies[-1].start()
+        for copy in copies:
+            copy.wait()
 
 
 def hold_kernel(*refs):
@@ -448,13 +461,20 @@
         ]
         if begins and ends:
             scratch += [pltpu.VMEM(each.shape, each.dtype) for each in (pick_shape, grid_shape, grid_shape)]
+        if ends and ready:
+            scratch += [
+                pltpu.VMEM(out_shape.shape, out_shape.dtype),
+                pltpu.SemaphoreType.DMA((batch,)),
+            ]
         return pl.pallas_call(
             functools.partial(
                 exchange_kernel, batch, points, owners, sizes, begins, ends, ready, shapes, where
             ),
             out_shape=out_shape,
             in_specs=[vmem] * (len(carried) + len(groups_in) + len(values)),
-            out_specs=jax.tree.map(lambda _: vmem, out_shape),
+            out_specs=jax.tree.map(
+                lambda _: pl.BlockSpec(memory_space=pl.ANY) if ends and ready else vmem, out_shape
+            ),
             scratch_shapes=scratch,
             cost_estimate=pl.CostEstimate(flops=5 * 10**9, bytes_accessed=4 * 2**20, transcendentals=0),
             compiler_params=pltpu.CompilerParams(vmem_limit_bytes=(24 if small else 50) * 2**20),

time: 21.4 us -> 21.4 us (level)
  no operation moved by 1% of the time
where the time goes in v7:
time: 21.4 us; the launch traced here: 21.3 us
  Pallas kernels  9.63 us (45%)
  starting transfers between devices  7.01 us (33%)
  waiting for transfers between devices  2.28 us (11%)
  local copies, waits for them, and re-layouts  0.86 us (4%)
  between operations  0.78 us (4%)
  other arithmetic  0.74 us (3%)
    pallas_call x3, Pallas kernels, call(): pl.pallas_call(functools.partial(exchange_kernel, batch, points, owners,...  8.64 us
    ppermute x4, starting transfers between devices, swap(): lax.ppermute(value, axis, [(at, partner(at) % count) for at in range(coun...  4.28 us
    ppermute x2, starting transfers between devices, rest_of_ring(): lax.ppermute(value, axis, [(at, (at + step) % count) for at in range(coun...  2.73 us
    ppermute x4, waiting for transfers between devices, swap(): lax.ppermute(value, axis, [(at, partner(at) % count) for at in range(coun...  2.27 us
    pallas_call x1, Pallas kernels, orbitals_of(): pl.pallas_call(functools.partial(orbitals_kernel, count, shapes, where),...  0.94 us
    unnamed x6, local copies, waits for them, and re-layouts  0.84 us
    convert_element_type x1, other arithmetic, shards(): jnp.where(position < stick_count[0], miller, -1).astype(jnp.float32)  0.69 us
  transfers between devices with their start and end apart: 6, of which 2 were waited for; matrix products, arithmetic and copies ran while one was open for 3% of the time, Pallas kernels for 27%

profile of v7, /device:TPU:1, one launch (start us, length us, event | category | flops | bytes accessed | tf_op | source)
XLA Modules:
  0.0 21.3 jit_solution(16524851260797528248)
XLA Ops:
  0.0 0.1 collective-permute-start.2
  0.1 2.7 %collective-permute-start.1 = (f32[96,128]{1,0:T(8,128)}, f32[96,128]{1,0:T(8,128)S(1)}, u32[]{:S(2)}, u32[]{:S(2)}) collective-permute-start(f32[96,128]{1,0:T(8,128)} %bitcast.20), channel_id=1, source_target_pairs={{0,16},{16,0},{1,17},{17,1},{2,18},{18,2},{3,19},{19,3},{4,20},{20... | collective-permute-start | bytes 147464 | tf_op jit(solution)/shard_map/ppermute | solution.py:415
  3.4 0.7 %select_convert_fusion = f32[2,128]{1,0:T(2,128)S(1)} fusion(s32[2,128]{1,0:T(2,128)} %param.5, pred[128]{0:T(512)(128)(4,1)S(1)} %iota_compare_fusion), kind=kLoop, calls=%fused_computation.5 | loop fusion | flops 512 | bytes 2176 | tf_op jit(solution)/shard_map/convert_element_type | solution.py:435
  4.1 0.0 slice-start
  4.1 0.0 copy-start
  4.1 0.0 slice-start.1
  4.1 0.1 collective-permute-start
  4.2 0.8 %copy-done = f32[1,2,48,128]{3,2,1,0:T(8,128)S(1)} copy-done((f32[1,2,48,128]{3,2,1,0:T(8,128)S(1)}, f32[1,2,48,128]{3,2,1,0:T(8,128)}, u32[]{:S(2)}) %copy-start) | copy-done | bytes 49176
  5.1 0.0 collective-permute-done.1
  5.1 0.5 %collective-permute-start.3 = (f32[96,128]{1,0:T(8,128)S(1)}, f32[96,128]{1,0:T(8,128)S(1)}, u32[]{:S(2)}, u32[]{:S(2)}) collective-permute-start(f32[96,128]{1,0:T(8,128)S(1)} %collective-permute-done.1), channel_id=1, source_target_pairs={{0,1},{1,0},{2,3},{3,2},{4,5},{5,4},{6,7},{7,6},{8,9},{9,8},{10,11... | collective-permute-start | bytes 147464 | tf_op jit(solution)/shard_map/ppermute | solution.py:409
  5.6 0.0 collective-permute-done.2
  5.6 0.9 %collective-permute-done.3 = f32[96,128]{1,0:T(8,128)S(1)} collective-permute-done((f32[96,128]{1,0:T(8,128)S(1)}, f32[96,128]{1,0:T(8,128)S(1)}, u32[]{:S(2)}, u32[]{:S(2)}) %collective-permute-start.3) | collective-permute-done | bytes 49184 | tf_op jit(solution)/shard_map/ppermute | solution.py:409
  6.5 1.8 %collective-permute-start.4 = (f32[2,2,96,128]{3,2,1,0:T(8,128)S(1)}, f32[2,2,96,128]{3,2,1,0:T(8,128)S(1)}, u32[]{:S(2)}, u32[]{:S(2)}) collective-permute-start(f32[2,2,96,128]{3,2,1,0:T(8,128)S(1)} %pad_maximum_fusion), channel_id=1, source_target_pairs={{0,15},{1,2},{2,1},{3,4},{4,3},{5,6},{6,5},{7,8},{8,7},{9,10},{10,... | collective-permute-start | bytes 589832 | tf_op jit(solution)/shard_map/ppermute | solution.py:409
  8.3 0.0 collective-permute-done.refs_1_
  8.3 0.0 slice-done
  8.3 0.0 slice-done.1
  8.4 3.3 %shard_map.48 = (bf16[320,256]{1,0:T(8,128)(2,1)S(1)}, f32[4,368,128]{2,1,0:T(8,128)S(1)}, f32[4,368,128]{2,1,0:T(8,128)S(1)}) custom-call(f32[8,128]{1,0:T(8,128)S(1)} %shard_map.46.refs_0_, f32[8,128]{1,0:T(8,128)S(1)} %collective-permute-done.refs_1_, f32[2,96,128]{2,1,0:T(8,128)S(1)} %get-tuple-element.18.refs_2_, ...), custom_call_target="tpu_custom_call" | custom-call | flops 5000000000 | bytes 4194304 | tf_op jit(solution)/shard_map/pallas_call | solution.py:469
  11.6 1.4 %collective-permute-done.4 = f32[2,2,96,128]{3,2,1,0:T(8,128)S(1)} collective-permute-done((f32[2,2,96,128]{3,2,1,0:T(8,128)S(1)}, f32[2,2,96,128]{3,2,1,0:T(8,128)S(1)}, u32[]{:S(2)}, u32[]{:S(2)}) %collective-permute-start.4) | collective-permute-done | bytes 196640 | tf_op jit(solution)/shard_map/ppermute | solution.py:409
  13.1 0.9 %shard_map.49 = (f32[4,368,128]{2,1,0:T(8,128)S(1)}, f32[4,368,128]{2,1,0:T(8,128)S(1)}) custom-call(bf16[320,256]{1,0:T(8,128)(2,1)S(1)} %get-tuple-element.10.pick_ref.refs_0_, f32[2,96,128]{2,1,0:T(8,128)S(1)} %get-tuple-element.16.refs_0_, f32[2,96,128]{2,1,0:T(8,128)S(1)} %get-tuple-element.15.refs_1_, bf16[3088,1152]{1,0:T(8,128)(2,1)S(1)} %bitcast.17), custom_call_target="tpu_custom_call" | custom-call | flops 1000000000 | bytes 1048576 | tf_op jit(solution)/shard_map/pallas_call | solution.py:485
  14.0 1.9 %collective-permute-start.5 = (f32[4,368,128]{2,1,0:T(8,128)S(1)}, f32[4,368,128]{2,1,0:T(8,128)S(1)}, u32[]{:S(2)}, u32[]{:S(2)}) collective-permute-start(f32[4,368,128]{2,1,0:T(8,128)S(1)} %get-tuple-element.13.refs_3_), channel_id=1, source_target_pairs={{0,1},{1,0},{2,3},{3,2},{4,5},{5,4},{6,7},{7,6},{8,9},{9,8},{10,11... | collective-permute-start | bytes 2261000 | tf_op jit(solution)/shard_map/ppermute | solution.py:409
  15.9 2.4 %shard_map.50.refs_2_ = f32[4,368,128]{2,1,0:T(8,128)S(1)} custom-call(bf16[320,256]{1,0:T(8,128)(2,1)S(1)} %get-tuple-element.10.pick_ref.refs_0_, f32[4,368,128]{2,1,0:T(8,128)S(1)} %get-tuple-element.11.refs_1_, f32[4,368,128]{2,1,0:T(8,128)S(1)} %get-tuple-element.12.refs_2_, f32[4,368,128]{2,1,0:T(8,128)S(1)} %get-tuple-element.13.refs_3_, ...), custom_call_target="tpu_custom_call" | custom-call | flops 5000000000 | bytes 4194304 | tf_op jit(solution)/shard_map/pallas_call | solution.py:469
  18.3 0.0 collective-permute-done.5.refs_3_
  18.4 2.9 %shard_map.51 = f32[96,128]{1,0:T(8,128)} custom-call(bf16[320,256]{1,0:T(8,128)(2,1)S(1)} %get-tuple-element.10.pick_ref.refs_0_, f32[4,368,128]{2,1,0:T(8,128)S(1)} %get-tuple-element.11.refs_1_, f32[4,368,128]{2,1,0:T(8,128)S(1)} %shard_map.50.refs_2_, f32[4,368,128]{2,1,0:T(8,128)S(1)} %collective-permute-done.5.refs_3_, bf16[3088,1152]{1,0:T(8,128)(2,1)S(1)} %bitcast.17), custom_call_target="tpu_custom_call" | custom-call | flops 5000000000 | bytes 4194304 | tf_op jit(solution)/shard_map/pallas_call | solution.py:469
  (9 shorter events, 0.1 us)
Async XLA Ops:
  0.0 5.6 %collective-permute-start.2 = (f32[96,128]{1,0:T(8,128)}, f32[96,128]{1,0:T(8,128)S(1)}, u32[]{:S(2)}, u32[]{:S(2)}) collective-permute-start(f32[96,128]{1,0:T(8,128)} %bitcast.19), channel_id=1, source_target_pairs={{0,1},{1,0},{2,3},{3,2},{4,5},{5,4},{6,7},{7,6},{8,9},{9,8},{10,11... | collective-permute-start | bytes 147464 | tf_op jit(solution)/shard_map/ppermute | solution.py:409
  0.1 5.0 %collective-permute-start.1 = (f32[96,128]{1,0:T(8,128)}, f32[96,128]{1,0:T(8,128)S(1)}, u32[]{:S(2)}, u32[]{:S(2)}) collective-permute-start(f32[96,128]{1,0:T(8,128)} %bitcast.20), channel_id=1, source_target_pairs={{0,16},{16,0},{1,17},{17,1},{2,18},{18,2},{3,19},{19,3},{4,20},{20... | collective-permute-start | bytes 147464 | tf_op jit(solution)/shard_map/ppermute | solution.py:415
  4.1 4.3 %slice-start = ((s8[7114752]{0:T(1024)(128)(4,1)}), s8[4194304]{0:T(1024)(128)(4,1)S(1)}, s32[]{:S(2)}) async-start(s8[7114752]{0:T(1024)(128)(4,1)} %bitcast.16), calls=%async_computation | async-start | bytes 8388608
  4.1 1.0 %copy-start = (f32[1,2,48,128]{3,2,1,0:T(8,128)S(1)}, f32[1,2,48,128]{3,2,1,0:T(8,128)}, u32[]{:S(2)}) copy-start(f32[1,2,48,128]{3,2,1,0:T(8,128)} %param.4) | copy-start | bytes 147460
  4.1 4.3 %slice-start.1 = ((s8[7114752]{0:T(1024)(128)(4,1)}), s8[2920448]{0:T(1024)(128)(4,1)S(1)}, s32[]{:S(2)}) async-start(s8[7114752]{0:T(1024)(128)(4,1)} %bitcast.16), calls=%async_computation.1 | async-start | bytes 5840896
  4.1 4.2 %collective-permute-start = (f32[8,128]{1,0:T(8,128)S(1)}, f32[8,128]{1,0:T(8,128)S(1)}, u32[]{:S(2)}, u32[]{:S(2)}) collective-permute-start(f32[8,128]{1,0:T(8,128)S(1)} %concatenate.3.refs_0_), channel_id=1, source_target_pairs={{0,16},{16,0},{1,17},{17,1},{2,18},{18,2},{3,19},{19,3},{4,20},{20... | collective-permute-start | bytes 12296 | tf_op jit(solution)/shard_map/ppermute | solution.py:415
  5.1 1.4 %collective-permute-start.3 = (f32[96,128]{1,0:T(8,128)S(1)}, f32[96,128]{1,0:T(8,128)S(1)}, u32[]{:S(2)}, u32[]{:S(2)}) collective-permute-start(f32[96,128]{1,0:T(8,128)S(1)} %collective-permute-done.1), channel_id=1, source_target_pairs={{0,1},{1,0},{2,3},{3,2},{4,5},{5,4},{6,7},{7,6},{8,9},{9,8},{10,11... | collective-permute-start | bytes 147464 | tf_op jit(solution)/shard_map/ppermute | solution.py:409
  6.5 6.5 %collective-permute-start.4 = (f32[2,2,96,128]{3,2,1,0:T(8,128)S(1)}, f32[2,2,96,128]{3,2,1,0:T(8,128)S(1)}, u32[]{:S(2)}, u32[]{:S(2)}) collective-permute-start(f32[2,2,96,128]{3,2,1,0:T(8,128)S(1)} %pad_maximum_fusion), channel_id=1, source_target_pairs={{0,15},{1,2},{2,1},{3,4},{4,3},{5,6},{6,5},{7,8},{8,7},{9,10},{10,... | collective-permute-start | bytes 589832 | tf_op jit(solution)/shard_map/ppermute | solution.py:409
  14.0 4.3 %collective-permute-start.5 = (f32[4,368,128]{2,1,0:T(8,128)S(1)}, f32[4,368,128]{2,1,0:T(8,128)S(1)}, u32[]{:S(2)}, u32[]{:S(2)}) collective-permute-start(f32[4,368,128]{2,1,0:T(8,128)S(1)} %get-tuple-element.13.refs_3_), channel_id=1, source_target_pairs={{0,1},{1,0},{2,3},{3,2},{4,5},{5,4},{6,7},{7,6},{8,9},{9,8},{10,11... | collective-permute-start | bytes 2261000 | tf_op jit(solution)/shard_map/ppermute | solution.py:409

commit v8 on v7

--- a/solution.py
+++ b/solution.py
@@ -97,10 +97,10 @@
             rows = round_up(many.shape[0], ROWS)
             depth = round_up(1 + np.flatnonzero(np.abs(many).max(axis=0) > 1e-9)[-1], ROWS)
         few_back = -few * place_weight * scale * (points / grid) ** 2
-        by_parity["synth"].append(split_columns(few.T * scale, n_place, n_picked))
+        by_parity["synth"].append(split_columns((few.T * scale)[:depth], depth, n_picked))
         by_parity["project"].append(split_columns(few_back, n_picked, n_place))
         by_parity["forward"].append(split_columns((many * place_weight)[:, :depth], rows, depth))
-        by_parity["inverse"].append(split_columns(many.T, n_place, rows))
+        by_parity["inverse"].append(split_columns(many.T[:depth], depth, rows))
 
     index = np.arange(points)
     angle = 2.0 * np.pi * ((index[:, None] * index[None, :]) % points) / points
@@ -200,6 +200,13 @@
     return out[:, :lanes] + out[:, lanes:]
 
 
+def fill_rows(value, rows):
+    missing = rows - value.shape[0]
+    if not missing:
+        return value
+    return jnp.concatenate([value, jnp.zeros((missing, value.shape[1]), value.dtype)], axis=0)
+
+
 def pick_matrix(indices, codes, points):
     first, second = indices[0:1], indices[1:2]
     alive = first >= 0.0
@@ -250,7 +257,7 @@
         coefs_ref[at] = coefs[at * rows : (at + 1) * rows]
 
     def body(at):
-        orbs_ref[at] = product(get("synth", at), coefs_ref[at])
+        orbs_ref[at] = fill_rows(product(get("synth", at), coefs_ref[at]), orbs_ref.shape[1])
 
     each_part(small, body)
     for at, quadrant in enumerate(unfold([orbs_ref[at] for at in range(4)])):
@@ -329,7 +336,7 @@
                 lambda at, part: product(get("forward", at), part[: get("forward", at).shape[1] // 3]),
                 lambda at, part: turn(part, turn_right) * weights[: part.shape[0]],
                 lambda at, part: turn(part, turn_right),
-                lambda at, part: product(get("inverse", at), part),
+                lambda at, part: fill_rows(product(get("inverse", at), part), visit[at].shape[0]),
             )
             potential = density
             for stage in stages:

time: 21.4 us -> 21.4 us (level)
  transfers between devices with their start and end apart: 6 -> 6, of which waited for: 2 -> 2; matrix products, arithmetic and copies ran while one was open for 3% -> 4% of each run, Pallas kernels for 27% -> 27%
where the time goes in v8:
time: 21.4 us; the launch traced here: 21.2 us
  Pallas kernels  9.57 us (45%)
  starting transfers between devices  7.01 us (33%)
  waiting for transfers between devices  2.27 us (11%)
  local copies, waits for them, and re-layouts  0.86 us (4%)
  between operations  0.78 us (4%)
  other arithmetic  0.74 us (3%)
    pallas_call x3, Pallas kernels, call(): pl.pallas_call(functools.partial(exchange_kernel, batch, points, owners,...  8.58 us
    ppermute x4, starting transfers between devices, swap(): lax.ppermute(value, axis, [(at, partner(at) % count) for at in range(coun...  4.28 us
    ppermute x2, starting transfers between devices, rest_of_ring(): lax.ppermute(value, axis, [(at, (at + step) % count) for at in range(coun...  2.73 us
    ppermute x4, waiting for transfers between devices, swap(): lax.ppermute(value, axis, [(at, partner(at) % count) for at in range(coun...  2.26 us
    pallas_call x1, Pallas kernels, orbitals_of(): pl.pallas_call(functools.partial(orbitals_kernel, count, shapes, where),...  0.93 us
    unnamed x6, local copies, waits for them, and re-layouts  0.84 us
    convert_element_type x1, other arithmetic, shards(): jnp.where(position < stick_count[0], miller, -1).astype(jnp.float32)  0.69 us
  transfers between devices with their start and end apart: 6, of which 2 were waited for; matrix products, arithmetic and copies ran while one was open for 4% of the time, Pallas kernels for 27%

profile of v8, /device:TPU:1, one launch (start us, length us, event | category | flops | bytes accessed | tf_op | source)
XLA Modules:
  0.0 21.2 jit_solution(689100868489638121)
XLA Ops:
  0.0 0.1 collective-permute-start.2
  0.1 2.7 %collective-permute-start.1 = (f32[96,128]{1,0:T(8,128)}, f32[96,128]{1,0:T(8,128)S(1)}, u32[]{:S(2)}, u32[]{:S(2)}) collective-permute-start(f32[96,128]{1,0:T(8,128)} %bitcast.20), channel_id=1, source_target_pairs={{0,16},{16,0},{1,17},{17,1},{2,18},{18,2},{3,19},{19,3},{4,20},{20... | collective-permute-start | bytes 147464 | tf_op jit(solution)/shard_map/ppermute | solution.py:422
  3.4 0.7 %select_convert_fusion = f32[2,128]{1,0:T(2,128)S(1)} fusion(s32[2,128]{1,0:T(2,128)} %param.5, pred[128]{0:T(512)(128)(4,1)S(1)} %iota_compare_fusion), kind=kLoop, calls=%fused_computation.5 | loop fusion | flops 512 | bytes 2176 | tf_op jit(solution)/shard_map/convert_element_type | solution.py:442
  4.1 0.0 slice-start
  4.1 0.0 copy-start
  4.1 0.0 slice-start.1
  4.1 0.1 collective-permute-start
  4.2 0.8 %copy-done = f32[1,2,48,128]{3,2,1,0:T(8,128)S(1)} copy-done((f32[1,2,48,128]{3,2,1,0:T(8,128)S(1)}, f32[1,2,48,128]{3,2,1,0:T(8,128)}, u32[]{:S(2)}) %copy-start) | copy-done | bytes 49176
  5.1 0.0 collective-permute-done.1
  5.1 0.5 %collective-permute-start.3 = (f32[96,128]{1,0:T(8,128)S(1)}, f32[96,128]{1,0:T(8,128)S(1)}, u32[]{:S(2)}, u32[]{:S(2)}) collective-permute-start(f32[96,128]{1,0:T(8,128)S(1)} %collective-permute-done.1), channel_id=1, source_target_pairs={{0,1},{1,0},{2,3},{3,2},{4,5},{5,4},{6,7},{7,6},{8,9},{9,8},{10,11... | collective-permute-start | bytes 147464 | tf_op jit(solution)/shard_map/ppermute | solution.py:416
  5.6 0.0 collective-permute-done.2
  5.7 0.9 %collective-permute-done.3 = f32[96,128]{1,0:T(8,128)S(1)} collective-permute-done((f32[96,128]{1,0:T(8,128)S(1)}, f32[96,128]{1,0:T(8,128)S(1)}, u32[]{:S(2)}, u32[]{:S(2)}) %collective-permute-start.3) | collective-permute-done | bytes 49184 | tf_op jit(solution)/shard_map/ppermute | solution.py:416
  6.5 1.8 %collective-permute-start.4 = (f32[2,2,96,128]{3,2,1,0:T(8,128)S(1)}, f32[2,2,96,128]{3,2,1,0:T(8,128)S(1)}, u32[]{:S(2)}, u32[]{:S(2)}) collective-permute-start(f32[2,2,96,128]{3,2,1,0:T(8,128)S(1)} %pad_maximum_fusion), channel_id=1, source_target_pairs={{0,15},{1,2},{2,1},{3,4},{4,3},{5,6},{6,5},{7,8},{8,7},{9,10},{10,... | collective-permute-start | bytes 589832 | tf_op jit(solution)/shard_map/ppermute | solution.py:416
  8.3 0.0 collective-permute-done.refs_1_
  8.3 0.0 slice-done
  8.3 0.0 slice-done.1
  8.4 3.3 %shard_map.48 = (bf16[320,256]{1,0:T(8,128)(2,1)S(1)}, f32[4,368,128]{2,1,0:T(8,128)S(1)}, f32[4,368,128]{2,1,0:T(8,128)S(1)}) custom-call(f32[8,128]{1,0:T(8,128)S(1)} %shard_map.46.refs_0_, f32[8,128]{1,0:T(8,128)S(1)} %collective-permute-done.refs_1_, f32[2,96,128]{2,1,0:T(8,128)S(1)} %get-tuple-element.18.refs_2_, ...), custom_call_target="tpu_custom_call" | custom-call | flops 5000000000 | bytes 4194304 | tf_op jit(solution)/shard_map/pallas_call | solution.py:476
  11.7 1.4 %collective-permute-done.4 = f32[2,2,96,128]{3,2,1,0:T(8,128)S(1)} collective-permute-done((f32[2,2,96,128]{3,2,1,0:T(8,128)S(1)}, f32[2,2,96,128]{3,2,1,0:T(8,128)S(1)}, u32[]{:S(2)}, u32[]{:S(2)}) %collective-permute-start.4) | collective-permute-done | bytes 196640 | tf_op jit(solution)/shard_map/ppermute | solution.py:416
  13.1 0.9 %shard_map.49 = (f32[4,368,128]{2,1,0:T(8,128)S(1)}, f32[4,368,128]{2,1,0:T(8,128)S(1)}) custom-call(bf16[320,256]{1,0:T(8,128)(2,1)S(1)} %get-tuple-element.10.pick_ref.refs_0_, f32[2,96,128]{2,1,0:T(8,128)S(1)} %get-tuple-element.16.refs_0_, f32[2,96,128]{2,1,0:T(8,128)S(1)} %get-tuple-element.15.refs_1_, bf16[3040,1152]{1,0:T(8,128)(2,1)S(1)} %bitcast.17), custom_call_target="tpu_custom_call" | custom-call | flops 1000000000 | bytes 1048576 | tf_op jit(solution)/shard_map/pallas_call | solution.py:492
  14.0 1.9 %collective-permute-start.5 = (f32[4,368,128]{2,1,0:T(8,128)S(1)}, f32[4,368,128]{2,1,0:T(8,128)S(1)}, u32[]{:S(2)}, u32[]{:S(2)}) collective-permute-start(f32[4,368,128]{2,1,0:T(8,128)S(1)} %get-tuple-element.13.refs_3_), channel_id=1, source_target_pairs={{0,1},{1,0},{2,3},{3,2},{4,5},{5,4},{6,7},{7,6},{8,9},{9,8},{10,11... | collective-permute-start | bytes 2261000 | tf_op jit(solution)/shard_map/ppermute | solution.py:416
  15.9 2.4 %shard_map.50.refs_2_ = f32[4,368,128]{2,1,0:T(8,128)S(1)} custom-call(bf16[320,256]{1,0:T(8,128)(2,1)S(1)} %get-tuple-element.10.pick_ref.refs_0_, f32[4,368,128]{2,1,0:T(8,128)S(1)} %get-tuple-element.11.refs_1_, f32[4,368,128]{2,1,0:T(8,128)S(1)} %get-tuple-element.12.refs_2_, f32[4,368,128]{2,1,0:T(8,128)S(1)} %get-tuple-element.13.refs_3_, ...), custom_call_target="tpu_custom_call" | custom-call | flops 5000000000 | bytes 4194304 | tf_op jit(solution)/shard_map/pallas_call | solution.py:476
  18.3 0.0 collective-permute-done.5.refs_3_
  18.3 2.9 %shard_map.51 = f32[96,128]{1,0:T(8,128)} custom-call(bf16[320,256]{1,0:T(8,128)(2,1)S(1)} %get-tuple-element.10.pick_ref.refs_0_, f32[4,368,128]{2,1,0:T(8,128)S(1)} %get-tuple-element.11.refs_1_, f32[4,368,128]{2,1,0:T(8,128)S(1)} %shard_map.50.refs_2_, f32[4,368,128]{2,1,0:T(8,128)S(1)} %collective-permute-done.5.refs_3_, bf16[3040,1152]{1,0:T(8,128)(2,1)S(1)} %bitcast.17), custom_call_target="tpu_custom_call" | custom-call | flops 5000000000 | bytes 4194304 | tf_op jit(solution)/shard_map/pallas_call | solution.py:476
  (9 shorter events, 0.1 us)
Async XLA Ops:
  0.0 5.6 %collective-permute-start.2 = (f32[96,128]{1,0:T(8,128)}, f32[96,128]{1,0:T(8,128)S(1)}, u32[]{:S(2)}, u32[]{:S(2)}) collective-permute-start(f32[96,128]{1,0:T(8,128)} %bitcast.19), channel_id=1, source_target_pairs={{0,1},{1,0},{2,3},{3,2},{4,5},{5,4},{6,7},{7,6},{8,9},{9,8},{10,11... | collective-permute-start | bytes 147464 | tf_op jit(solution)/shard_map/ppermute | solution.py:416
  0.1 5.0 %collective-permute-start.1 = (f32[96,128]{1,0:T(8,128)}, f32[96,128]{1,0:T(8,128)S(1)}, u32[]{:S(2)}, u32[]{:S(2)}) collective-permute-start(f32[96,128]{1,0:T(8,128)} %bitcast.20), channel_id=1, source_target_pairs={{0,16},{16,0},{1,17},{17,1},{2,18},{18,2},{3,19},{19,3},{4,20},{20... | collective-permute-start | bytes 147464 | tf_op jit(solution)/shard_map/ppermute | solution.py:422
  4.1 4.3 %slice-start = ((s8[7004160]{0:T(1024)(128)(4,1)}), s8[4194304]{0:T(1024)(128)(4,1)S(1)}, s32[]{:S(2)}) async-start(s8[7004160]{0:T(1024)(128)(4,1)} %bitcast.16), calls=%async_computation | async-start | bytes 8388608
  4.1 1.0 %copy-start = (f32[1,2,48,128]{3,2,1,0:T(8,128)S(1)}, f32[1,2,48,128]{3,2,1,0:T(8,128)}, u32[]{:S(2)}) copy-start(f32[1,2,48,128]{3,2,1,0:T(8,128)} %param.4) | copy-start | bytes 147460
  4.1 4.3 %slice-start.1 = ((s8[7004160]{0:T(1024)(128)(4,1)}), s8[2809856]{0:T(1024)(128)(4,1)S(1)}, s32[]{:S(2)}) async-start(s8[7004160]{0:T(1024)(128)(4,1)} %bitcast.16), calls=%async_computation.1 | async-start | bytes 5619712
  4.1 4.2 %collective-permute-start = (f32[8,128]{1,0:T(8,128)S(1)}, f32[8,128]{1,0:T(8,128)S(1)}, u32[]{:S(2)}, u32[]{:S(2)}) collective-permute-start(f32[8,128]{1,0:T(8,128)S(1)} %concatenate.3.refs_0_), channel_id=1, source_target_pairs={{0,16},{16,0},{1,17},{17,1},{2,18},{18,2},{3,19},{19,3},{4,20},{20... | collective-permute-start | bytes 12296 | tf_op jit(solution)/shard_map/ppermute | solution.py:422
  5.1 1.4 %collective-permute-start.3 = (f32[96,128]{1,0:T(8,128)S(1)}, f32[96,128]{1,0:T(8,128)S(1)}, u32[]{:S(2)}, u32[]{:S(2)}) collective-permute-start(f32[96,128]{1,0:T(8,128)S(1)} %collective-permute-done.1), channel_id=1, source_target_pairs={{0,1},{1,0},{2,3},{3,2},{4,5},{5,4},{6,7},{7,6},{8,9},{9,8},{10,11... | collective-permute-start | bytes 147464 | tf_op jit(solution)/shard_map/ppermute | solution.py:416
  6.5 6.5 %collective-permute-start.4 = (f32[2,2,96,128]{3,2,1,0:T(8,128)S(1)}, f32[2,2,96,128]{3,2,1,0:T(8,128)S(1)}, u32[]{:S(2)}, u32[]{:S(2)}) collective-permute-start(f32[2,2,96,128]{3,2,1,0:T(8,128)S(1)} %pad_maximum_fusion), channel_id=1, source_target_pairs={{0,15},{1,2},{2,1},{3,4},{4,3},{5,6},{6,5},{7,8},{8,7},{9,10},{10,... | collective-permute-start | bytes 589832 | tf_op jit(solution)/shard_map/ppermute | solution.py:416
  14.0 4.3 %collective-permute-start.5 = (f32[4,368,128]{2,1,0:T(8,128)S(1)}, f32[4,368,128]{2,1,0:T(8,128)S(1)}, u32[]{:S(2)}, u32[]{:S(2)}) collective-permute-start(f32[4,368,128]{2,1,0:T(8,128)S(1)} %get-tuple-element.13.refs_3_), channel_id=1, source_target_pairs={{0,1},{1,0},{2,3},{3,2},{4,5},{5,4},{6,7},{7,6},{8,9},{9,8},{10,11... | collective-permute-start | bytes 2261000 | tf_op jit(solution)/shard_map/ppermute | solution.py:416
